TPU v7x, 512 devices: a whole 4x8x8 slice. The times are simulated.
512 devices in a mesh: dp: 4 (over z_hi), seq: 64 (over z_lo, y, x), chan: 2 (over core).
Axes of the slice: x: 4, y: 8, z: 8 (z_hi: 4, z_lo: 2; z = z_hi * 2 + z_lo), core: 2. Of those that a mesh axis runs over, the one named last changes fastest.
Arguments:
- signal: bfloat16 [4, 8192, 512], P('dp', 'seq', 'chan'), may hold values from -6 to 6
- gating: bfloat16 [4, 8192, 512], P('dp', 'seq', 'chan'), may hold values from -6 to 6
- cotangent: bfloat16 [4, 8192, 8192], P('dp', 'seq', 'chan'), may hold values from -6 to 6
- filt: float32 [8192, 512], P('seq', 'chan'), may hold values from -1 to 1
- skip: float32 [512], P('chan'), may hold values from -3 to 3
- output_projection: bfloat16 [512, 8192], P('chan', 'dp'), may hold values from -0.0625 to 0.0625
- adapter_down_bank: bfloat16 [2, 512, 16], P(None, 'chan'), may hold values from -0.25 to 0.25
- adapter_up_bank: bfloat16 [2, 16, 8192], P(None, None, 'chan'), may hold values from -0.0625 to 0.0625
- adapter_index: int32 [4], P('dp'), may hold values from 0 to 1
- sequence_rank: int32 [4], P('dp'), may hold values from 1 to 16, as said below
- real_length: int32 [4], P('dp'), may hold values from 4096 to 8192, as said below
Outputs:
- grad_signal: bfloat16 [4, 8192, 512], P('dp', 'seq', 'chan')
- grad_gating: bfloat16 [4, 8192, 512], P('dp', 'seq', 'chan')
- grad_filt: float32 [8192, 512], P('seq', 'chan')
- grad_skip: float32 [512], P('chan')
- grad_a: float32 [2, 512, 16], P(None, 'chan')
- grad_b: float32 [2, 16, 8192], P(None, None, 'chan')
Inputs may be any that keep to these rules, and one draw needn't show every extreme that they name: `sequence_rank`: the first sequence uses all 16 ranks. Positions from real_length on are padding; the first sequence has none.
All inputs are finite; a program needn't handle non-finite values.
Results may differ from a plain program's by a relative error of at most 0.0052.
Values may be sent and summed in bfloat16 or wider, within the bound.
A program may use at most 64 MiB of HBM per device.

v0:
```python
import math

import jax
import jax.numpy as jnp
from jax import lax
from jax.sharding import PartitionSpec as P

ADAPTER_SCALE = 2.0
HIGHEST_PRECISION = lax.Precision.HIGHEST


def angle_table(row_index, col_index, period):
    product = row_index[:, None] * col_index[None, :] % period
    phase = product.astype(jnp.float32) * (2.0 * math.pi / period)
    return (jnp.cos(phase), jnp.sin(phase))


def blocks_forward(blocks_data):
    count = blocks_data.shape[0]
    cosine, sine = angle_table(
        jnp.arange(2 * count, dtype=jnp.int32), jnp.arange(count, dtype=jnp.int32), 2 * count
    )
    real_part = jnp.einsum("kn,nqc->kqc", cosine, blocks_data, precision=HIGHEST_PRECISION)
    imag_part = -jnp.einsum("kn,nqc->kqc", sine, blocks_data, precision=HIGHEST_PRECISION)
    return (real_part, imag_part)


def twiddle(real_part, imag_part, offsets, period, direction):
    cosine, sine = angle_table(jnp.arange(real_part.shape[0], dtype=jnp.int32), offsets, period)
    cosine = cosine[:, :, None]
    sine = sine[:, :, None]
    return (
        real_part * cosine + direction * imag_part * sine,
        imag_part * cosine - direction * real_part * sine,
    )


def offsets_section(real_part, imag_part, direction):
    grid = jnp.arange(real_part.shape[1], dtype=jnp.int32)
    cosine, sine = angle_table(grid, grid, real_part.shape[1])

    def apply_table(table, values):
        return jnp.einsum("jn,knc->kjc", table, values, precision=HIGHEST_PRECISION)

    return (
        apply_table(cosine, real_part) + direction * apply_table(sine, imag_part),
        apply_table(cosine, imag_part) - direction * apply_table(sine, real_part),
    )


def blocks_inverse(real_part, imag_part, period):
    count = real_part.shape[0]
    cosine, sine = angle_table(
        jnp.arange(count // 2, dtype=jnp.int32), jnp.arange(count, dtype=jnp.int32), count
    )
    first = jnp.einsum("nk,kqc->nqc", cosine, real_part, precision=HIGHEST_PRECISION)
    second = jnp.einsum("nk,kqc->nqc", sine, imag_part, precision=HIGHEST_PRECISION)
    return (first - second) / period


def spectral_products(spec_signal, spec_filter, spec_grad):
    signal_re, signal_im = spec_signal
    filter_re, filter_im = spec_filter
    grad_re, grad_im = spec_grad
    conv = (
        signal_re * filter_re - signal_im * filter_im,
        signal_re * filter_im + signal_im * filter_re,
    )
    corr_filter = (
        grad_re * filter_re + grad_im * filter_im,
        grad_im * filter_re - grad_re * filter_im,
    )
    corr_signal = (
        grad_re * signal_re + grad_im * signal_im,
        grad_im * signal_re - grad_re * signal_im,
    )
    return (conv, corr_filter, corr_signal)


def local(
    signal,
    gating,
    cotangent,
    filt,
    skip,
    output_projection,
    adapter_down_bank,
    adapter_up_bank,
    adapter_index,
    sequence_rank,
    real_length,
):
    seq_count = lax.axis_size("seq")
    seq_index = lax.axis_index("seq")
    length_dev = signal.shape[1]
    width_dev = signal.shape[2]
    quarter = length_dev // seq_count
    period = 2 * length_dev * seq_count
    source = signal[0].astype(jnp.float32)
    gate_row = gating[0].astype(jnp.float32)
    positions = seq_index * length_dev + jnp.arange(length_dev, dtype=jnp.int32)
    live = positions < real_length[0]
    masked = jnp.where(live[:, None], cotangent[0], jnp.zeros_like(cotangent[0]))
    selected_values = jnp.arange(adapter_down_bank.shape[0], dtype=jnp.int32) == adapter_index[0]
    selected_halfway = selected_values.astype(jnp.bfloat16)
    chosen_down_maps = jnp.einsum(
        "v,vxe->xe", selected_halfway, adapter_down_bank, preferred_element_type=jnp.float32
    ).astype(jnp.bfloat16)
    chosen_up_maps = jnp.einsum(
        "v,vjd->jd", selected_halfway, adapter_up_bank, preferred_element_type=jnp.float32
    ).astype(jnp.bfloat16)
    rank_mask = (jnp.arange(adapter_down_bank.shape[2], dtype=jnp.int32) < sequence_rank[0]).astype(
        jnp.float32
    )
    whole_weight = lax.all_gather(output_projection, "dp", axis=1, tiled=True)
    grad_main = lax.dot_general(
        lax.all_gather(masked, "chan", axis=1, tiled=True),
        whole_weight,
        (((1,), (1,)), ((), ())),
        preferred_element_type=jnp.float32,
    )
    down_part = lax.dot_general(
        masked, chosen_up_maps, (((1,), (1,)), ((), ())), preferred_element_type=jnp.float32
    )
    down_projected = lax.psum(down_part, "chan")
    backward_rank = (ADAPTER_SCALE * down_projected * rank_mask).astype(jnp.bfloat16)
    grad_y = grad_main + lax.dot_general(
        backward_rank,
        chosen_down_maps,
        (((1,), (1,)), ((), ())),
        preferred_element_type=jnp.float32,
    )
    grad_u = grad_y * gate_row
    regrouped = (
        lax.all_to_all(source, "seq", split_axis=0, concat_axis=0, tiled=True),
        lax.all_to_all(filt, "seq", split_axis=0, concat_axis=0, tiled=True),
        lax.all_to_all(grad_u, "seq", split_axis=0, concat_axis=0, tiled=True),
    )
    offsets = seq_index * quarter + jnp.arange(quarter, dtype=jnp.int32)
    halves = []
    for block_item in regrouped:
        real_part, imag_part = blocks_forward(block_item.reshape(seq_count, quarter, width_dev))
        real_part, imag_part = twiddle(real_part, imag_part, offsets, period, 1.0)
        halves.append(real_part)
        halves.append(imag_part)
    residues = (
        lax.all_to_all(halves[0], "seq", split_axis=0, concat_axis=1, tiled=True),
        lax.all_to_all(halves[1], "seq", split_axis=0, concat_axis=1, tiled=True),
        lax.all_to_all(halves[2], "seq", split_axis=0, concat_axis=1, tiled=True),
        lax.all_to_all(halves[3], "seq", split_axis=0, concat_axis=1, tiled=True),
        lax.all_to_all(halves[4], "seq", split_axis=0, concat_axis=1, tiled=True),
        lax.all_to_all(halves[5], "seq", split_axis=0, concat_axis=1, tiled=True),
    )
    spectra = [
        offsets_section(residues[0], residues[1], 1.0),
        offsets_section(residues[2], residues[3], 1.0),
        offsets_section(residues[4], residues[5], 1.0),
    ]
    products = spectral_products(spectra[0], spectra[1], spectra[2])
    partials = []
    for product_item in products:
        real_part, imag_part = offsets_section(product_item[0], product_item[1], -1.0)
        partials.append(real_part)
        partials.append(imag_part)
    back_blocks = (
        lax.all_to_all(partials[0], "seq", split_axis=1, concat_axis=0, tiled=True),
        lax.all_to_all(partials[1], "seq", split_axis=1, concat_axis=0, tiled=True),
        lax.all_to_all(partials[2], "seq", split_axis=1, concat_axis=0, tiled=True),
        lax.all_to_all(partials[3], "seq", split_axis=1, concat_axis=0, tiled=True),
        lax.all_to_all(partials[4], "seq", split_axis=1, concat_axis=0, tiled=True),
        lax.all_to_all(partials[5], "seq", split_axis=1, concat_axis=0, tiled=True),
    )
    results = []
    for pair_index in range(3):
        real_part, imag_part = twiddle(
            back_blocks[2 * pair_index], back_blocks[2 * pair_index + 1], offsets, period, -1.0
        )
        results.append(blocks_inverse(real_part, imag_part, period).reshape(length_dev, width_dev))
    conv, corr_filter, corr_signal = (
        lax.all_to_all(results[0], "seq", split_axis=0, concat_axis=0, tiled=True),
        lax.all_to_all(results[1], "seq", split_axis=0, concat_axis=0, tiled=True),
        lax.all_to_all(results[2], "seq", split_axis=0, concat_axis=0, tiled=True),
    )
    inner = conv + skip * source
    gated = (gate_row * inner).astype(jnp.bfloat16)
    grad_gating = (grad_y * inner).astype(jnp.bfloat16)
    grad_signal = (corr_filter + skip * grad_u).astype(jnp.bfloat16)
    grad_filt = lax.psum(corr_signal, "dp")
    up_part = jnp.dot(gated, chosen_down_maps, preferred_element_type=jnp.float32)
    up_projected = lax.psum(up_part, "chan")
    forward_rank = (ADAPTER_SCALE * up_projected * rank_mask).astype(jnp.bfloat16)
    picked_full = selected_values.astype(jnp.float32)
    a_term = lax.dot_general(
        gated, backward_rank, (((0,), (0,)), ((), ())), preferred_element_type=jnp.float32
    )
    b_term = lax.dot_general(
        forward_rank, masked, (((0,), (0,)), ((), ())), preferred_element_type=jnp.float32
    )
    a_bank = picked_full[:, None, None] * a_term[None]
    b_bank = picked_full[:, None, None] * b_term[None]
    skip_term = jnp.sum(grad_u * source, axis=0)
    grad_a, grad_b, grad_skip = lax.psum((a_bank, b_bank, skip_term), ("dp", "seq"))
    return (grad_signal[None], grad_gating[None], grad_filt, grad_skip, grad_a, grad_b)


def solution(mesh):
    placed = (
        P("dp", "seq", "chan"),
        P("dp", "seq", "chan"),
        P("dp", "seq", "chan"),
        P("seq", "chan"),
        P("chan"),
        P("chan", "dp"),
        P(None, "chan", None),
        P(None, None, "chan"),
        P("dp"),
        P("dp"),
        P("dp"),
    )
    return jax.shard_map(
        local,
        mesh=mesh,
        in_specs=placed,
        out_specs=(
            P("dp", "seq", "chan"),
            P("dp", "seq", "chan"),
            P("seq", "chan"),
            P("chan"),
            P(None, "chan", None),
            P(None, None, "chan"),
        ),
        check_vma=False,
    )
```

profile of v0, /device:TPU:6, one launch (start us, length us, event | category | flops | bytes accessed | tf_op | source)
XLA Modules:
  0.0 1788.2 jit_solution(18429649351473932163)
XLA Ops:
  9.6 12.4 all-to-all-start.9
  32.0 6.2 all-to-all-start.3
  39.3 8.9 all-to-all-done.3
  50.3 5.7 all-to-all-start.4
  56.9 10.5 all-to-all-done.4
  74.4 9.5 all-to-all-done.5
  90.3 10.4 all-to-all-done.10
  100.7 5.7 all-to-all-start.11
  107.3 11.9 all-to-all-done.11
  127.3 14.4 all-to-all-start.12
  143.9 21.7 %all-to-all-done.12 = f32[2,128,256]{2,0,1:T(2,128)S(1)} async-done(((f32[2,128,256]{2,0,1:T(2,128)}), f32[2,128,256]{2,0,1:T(2,128)S(1)}, u32[]{:S(2)}, u32[]{:S(2)}) %all-to-all-start.12) | async-done | bytes 262176 | tf_op jit(solution)/shard_map/all_to_all | solution.py:166
  165.5 9.5 all-to-all-start.13
  177.1 10.4 all-to-all-done.13
  189.5 5.4 all-to-all-start.14
  195.5 9.4 all-to-all-done.14
  209.8 5.6 fusion.59
  215.4 15.7 all_to_all.267
  233.2 5.5 all-to-all-start.1
  239.6 11.0 all-to-all-done.1
  250.6 5.7 all-to-all-start.2
  257.2 10.4 all-to-all-done.2
  280.3 9.1 all-to-all-done.15
  289.5 5.4 all-to-all-start.16
  297.0 9.1 all-to-all-done.16
  306.1 5.4 all-to-all-start.6
  314.6 8.1 all-to-all-done.6
  331.7 7.8 all-to-all-done.7
  339.5 5.4 all-to-all-start.17
  346.9 8.3 all-to-all-done.17
  355.2 5.6 all-to-all-start.8
  361.2 1355.3 %all-reduce = (f32[256]{0:T(256)}, f32[2,256,16]{1,2,0:T(8,128)}) all-reduce(f32[256]{0:T(256)S(1)} %copy-done.9, f32[2,256,16]{1,2,0:T(8,128)S(1)} %broadcast_multiply_fusion.1), channel_id=1, replica_groups=mesh['dp'=4,'seq'=64,'chan'=2] {'dp','seq'}, use_global_device_ids=true, to_apply=%region_3.4 | all-reduce | flops 8448 | bytes 67584 | tf_op jit(solution)/shard_map/psum | solution.py:202
  1718.0 59.1 %all-reduce.5.cloned.1.call-done = f32[128,256]{1,0:T(8,128)} async-done(((f32[128,256]{1,0:T(8,128)}), f32[128,256]{1,0:T(8,128)}) %all-reduce.5.cloned.1.call-update) | async-done | bytes 131088 | tf_op jit(solution)/shard_map/psum | solution.py:188
  (147 shorter events, 85.1 us)
Async XLA Ops:
  8.0 168.5 %copy-start = (bf16[2,16,4096]{2,1,0:T(8,128)(2,1)S(1)}, bf16[2,16,4096]{2,1,0:T(8,128)(2,1)}, u32[]{:S(2)}) copy-start(bf16[2,16,4096]{2,1,0:T(8,128)(2,1)} %param.18) | copy-start | bytes 786436
  9.6 22.4 %all-to-all-start.9 = ((f32[64,2,256]{2,1,0:T(2,128)}), f32[64,2,256]{2,1,0:T(2,128)S(1)}, u32[]{:S(2)}, u32[]{:S(2)}) async-start(f32[64,2,256]{2,1,0:T(2,128)} %reshape.117), calls=%async_computation.9 | async-start | bytes 262144 | tf_op jit(solution)/shard_map/all_to_all | solution.py:135
  22.0 187.4 %all-gather.3.cloned.1.call-start = ((), (), s32[]{:S(2)}) async-start(), calls=%async_computation.18 | async-start | bytes 3145728 | tf_op jit(solution)/shard_map/all_gather | solution.py:117
  32.0 16.2 all-to-all-start.3
  50.3 17.1 all-to-all-start.4
  67.4 16.6 all-to-all-start.5
  72.7 137.1 %all-gather.5.cloned.1.call-start = ((), (), s32[]{:S(2)}) async-start(), calls=%async_computation.19 | async-start | bytes 5242880 | tf_op jit(solution)/shard_map/all_gather | solution.py:115
  83.9 16.7 all-to-all-start.10
  100.7 18.5 %all-to-all-start.11 = ((f32[128,2,256]{2,1,0:T(2,128)}), f32[128,2,256]{2,1,0:T(2,128)S(1)}, u32[]{:S(2)}, u32[]{:S(2)}) async-start(f32[128,2,256]{2,1,0:T(2,128)} %copy.99), calls=%async_computation.11 | async-start | bytes 524288 | tf_op jit(solution)/shard_map/all_to_all | solution.py:148
  122.6 53.8 %copy-start.13 = (bf16[2,256,16]{1,2,0:T(8,128)(2,1)S(1)}, bf16[2,256,16]{1,2,0:T(8,128)(2,1)}, u32[]{:S(2)}) copy-start(bf16[2,256,16]{1,2,0:T(8,128)(2,1)} %param.17) | copy-start | bytes 49156
  127.3 67.8 %copy-start.1 = (bf16[128,4096]{1,0:T(8,128)(2,1)S(1)}, bf16[128,4096]{1,0:T(8,128)(2,1)}, u32[]{:S(2)}) copy-start(bf16[128,4096]{1,0:T(8,128)(2,1)} %bitcast_select_fusion) | copy-start | bytes 3145732
  127.3 38.3 %all-to-all-start.12 = ((f32[2,128,256]{2,0,1:T(2,128)}), f32[2,128,256]{2,0,1:T(2,128)S(1)}, u32[]{:S(2)}, u32[]{:S(2)}) async-start(f32[2,128,256]{2,0,1:T(2,128)} %copy.104), calls=%async_computation.12 | async-start | bytes 524288 | tf_op jit(solution)/shard_map/all_to_all | solution.py:166
  142.3 62.7 %copy-start.2 = (bf16[1,128,256]{2,1,0:T(8,128)(2,1)S(1)}, bf16[1,128,256]{2,1,0:T(8,128)(2,1)}, u32[]{:S(2)}) copy-start(bf16[1,128,256]{2,1,0:T(8,128)(2,1)} %param.11) | copy-start | bytes 196612
  142.3 62.7 %copy-start.3 = (bf16[1,128,256]{2,1,0:T(8,128)(2,1)S(1)}, bf16[1,128,256]{2,1,0:T(8,128)(2,1)}, u32[]{:S(2)}) copy-start(bf16[1,128,256]{2,1,0:T(8,128)(2,1)} %param.12) | copy-start | bytes 196612
  142.3 62.7 %copy-start.6 = (f32[256]{0:T(256)S(1)}, f32[256]{0:T(256)}, u32[]{:S(2)}) copy-start(f32[256]{0:T(256)} %param.15) | copy-start | bytes 3076
  165.5 22.0 %all-to-all-start.13 = ((f32[2,128,256]{2,0,1:T(2,128)}), f32[2,128,256]{2,0,1:T(2,128)S(1)}, u32[]{:S(2)}, u32[]{:S(2)}) async-start(f32[2,128,256]{2,0,1:T(2,128)} %copy.106), calls=%async_computation.13 | async-start | bytes 524288 | tf_op jit(solution)/shard_map/all_to_all | solution.py:167
  189.5 15.4 all-to-all-start.14
  233.2 17.4 all-to-all-start.1
  250.6 17.0 all-to-all-start.2
  270.8 40.8 %copy-start.11 = (f32[16]{0:T(128)S(1)}, f32[16]{0:T(128)}, u32[]{:S(2)}) copy-start(f32[16]{0:T(128)} %copy-done.10) | copy-start | bytes 196
  272.9 16.6 all-to-all-start.15
  289.5 16.6 all-to-all-start.16
  306.1 16.7 all-to-all-start.6
  322.8 16.7 all-to-all-start.7
  328.2 1389.8 %all-reduce.7.cloned.1.call-start = ((), (), s32[]{:S(2)}) async-start(), calls=%async_computation.21 | async-start | bytes 1048576 | tf_op jit(solution)/shard_map/psum | solution.py:202
  329.2 31.7 %copy-start.5 = (bf16[128,256]{1,0:T(8,128)(2,1)S(1)}, bf16[128,256]{1,0:T(8,128)(2,1)}, u32[]{:S(2)}) copy-start(bf16[128,256]{1,0:T(8,128)(2,1)} %copy-done.4) | copy-start | bytes 196612
  329.2 31.7 %copy-start.8 = (f32[128,16]{0,1:T(8,128)S(1)}, f32[128,16]{0,1:T(8,128)}, u32[]{:S(2)}) copy-start(f32[128,16]{0,1:T(8,128)} %copy-done.7) | copy-start | bytes 24580
  329.2 31.7 %copy-start.12 = (f32[16]{0:T(128)S(1)}, f32[16]{0:T(128)}, u32[]{:S(2)}) copy-start(f32[16]{0:T(128)} %copy-done.10) | copy-start | bytes 196
  329.2 32.0 %copy-start.9 = (f32[256]{0:T(256)S(1)}, f32[256]{0:T(256)}, u32[]{:S(2)}) copy-start(f32[256]{0:T(256)} %get-tuple-element.10) | copy-start | bytes 3076
  339.5 15.8 all-to-all-start.17
  355.2 1362.0 %all-to-all-start.8 = ((f32[64,2,256]{2,1,0:T(2,128)}), f32[64,2,256]{2,1,0:T(2,128)S(1)}, u32[]{:S(2)}, u32[]{:S(2)}) async-start(f32[64,2,256]{2,1,0:T(2,128)} %copy.93), calls=%async_computation.8 | async-start | bytes 262144 | tf_op jit(solution)/shard_map/all_to_all | solution.py:181
  360.8 1416.2 %all-reduce.5.cloned.1.call-start = ((), (), s32[]{:S(2)}) async-start(), calls=%async_computation.20 | async-start | bytes 262144 | tf_op jit(solution)/shard_map/psum | solution.py:188
  (3 other events, 19.5 us)
Sparse Core Ops, SparseCore 0:
  25.2 22.1 all-gather.2
  75.7 99.4 all-gather.4
Sparse Core Ops, SparseCore 1:
  334.3 231.4 all-reduce.6
  1717.3 59.7 all-reduce.4
where the time goes:
time: 1800 us; the launch traced here: 1790 us
  blocking collectives  1370 us (76%)
  waiting for transfers between devices  221 us (12%)
  starting transfers between devices  114 us (6%)
  matrix products  31.1 us (2%)
  local copies, waits for them, and re-layouts  24 us (1%)
  between operations  18.5 us (1%)
    psum x1, blocking collectives, local(): lax.psum((a_bank, b_bank, skip_term), ('dp', 'seq'))  1360 us
    psum x1, waiting for transfers between devices, local(): grad_filt = lax.psum(corr_signal, 'dp')  59.1 us
  transfers between devices with their start and end apart: 21, of which 17 were waited for; matrix products, arithmetic and copies ran while one was open for 2% of the time, Pallas kernels for 0%

commit v1 on v0

v1 whole, which is shorter than its diff:
```python
import functools
import math

import jax
import jax.numpy as jnp
import ml_dtypes
import numpy as np
from jax import lax
from jax.experimental import pallas as pl
from jax.experimental.pallas import tpu as pltpu
from jax.sharding import PartitionSpec as P

MESH = pl.DeviceIdType.MESH
BF = jnp.bfloat16
F32 = jnp.float32
LANES = 128
PER = 4
HALF_ROWS = 8


def split3(table, axis, order):
    high = table.astype(ml_dtypes.bfloat16)
    low = (table - high.astype(np.float64)).astype(ml_dtypes.bfloat16)
    return np.concatenate([high if o else low for o in order], axis=axis)


def tables(n):
    rows = -(-(n + 1) // 8) * 8
    k1 = np.arange(rows)
    used = (k1 <= n).astype(np.float64)
    i = np.arange(n)
    a = np.arange(LANES)
    period = 2 * n * LANES
    th1 = 2 * math.pi * (k1[:, None] * i[None, :] % (2 * n)) / (2 * n)
    first = np.concatenate([np.cos(th1) * used[:, None], -np.sin(th1) * used[:, None]], 0)
    thw = 2 * math.pi * (k1[:, None] * a[None, :] % period) / period
    tw_cos, tw_sin = np.cos(thw), np.sin(thw)
    th2 = 2 * math.pi * (a[:, None] * a[None, :] % LANES) / LANES
    c2, s2 = np.cos(th2), np.sin(th2)
    second = np.block([[c2, -s2], [s2, c2]])
    second_back = np.block([[c2, s2], [-s2, c2]])
    weight = used * np.where((k1 == 0) | (k1 == n), 1.0, 2.0) / period
    last = np.concatenate([np.cos(th1).T * weight, -np.sin(th1).T * weight], 1)
    return (
        split3(first, 1, (1, 1, 0)),
        split3(second, 0, (1, 1, 0)),
        split3(second_back, 0, (1, 1, 0)),
        split3(last, 1, (1, 1, 0)),
        tw_cos.astype(np.float32),
        tw_sin.astype(np.float32),
    )


def split_data(x, axis):
    high = x.astype(BF)
    low = (x - high.astype(F32)).astype(BF)
    return jnp.concatenate([high, low, high], axis=axis)


def dot(a, b):
    return jnp.dot(a, b, preferred_element_type=F32)


def dot_t(a, b):
    return lax.dot_general(a, b, (((1,), (1,)), ((), ())), preferred_element_type=F32)


def dot_0(a, b):
    return lax.dot_general(a, b, (((0,), (0,)), ((), ())), preferred_element_type=F32)


def kernel(
    n,
    index_ref, rank_ref, length_ref,
    signal_ref, gating_ref, cot_ref, filt_ref, skip_ref, w_ref, down_ref, up_ref,
    t1_ref, t2_ref, t2b_ref, t1b_ref, tc_ref, ts_ref,
    gsig_ref, ggat_ref, gfilt_ref, gskip_ref, ga_ref, gb_ref,
    masked, sig_t, gate_t, grady_t, spec_s, spec_f, spec_g,
    sf_send, sf_recv, c_send, c_recv, u_send, u_recv, k_send, k_recv,
    m_recv, w_recv, pre_send, pre_recv, own_part, ret_send, ret_recv,
    d_send, d_recv, r_send, r_recv,
    b_send, b_recv, q_send, q_recv, g_send, g_recv, f_send, f_recv,
    a2a_send_sem, a2a_recv_sem, m_send_sem, m_recv_sem, w_sem, pre_send_sem, pre_recv_sem,
    ret_send_sem, ret_recv_sem, d_sem, r_sem, b_sem, q_send_sem, q_recv_sem, g_sem,
    f_send_sem, f_recv_sem,
):
    dp = lax.axis_index("dp")
    me = lax.axis_index("seq")
    ch = lax.axis_index("chan")
    other = 1 - ch
    width = w_ref.shape[0]
    cols = w_ref.shape[1] // 2
    half = cot_ref.shape[1]
    n_own = b_send.shape[1] // LANES
    rows = t1_ref.shape[0] // 2
    up_chunks = half // LANES
    a_chunks = -(-width // LANES)

    barrier = pltpu.get_barrier_semaphore()

    def greet(d, _):
        pl.semaphore_signal(
            barrier, inc=1, device_id=(dp, lax.rem(me + d, n), ch), device_id_type=MESH
        )
        return 0

    lax.fori_loop(1, n, greet, 0)
    for d in range(4):
        for c in range(2):
            if d or c:
                pl.semaphore_signal(
                    barrier, inc=1, device_id=(lax.rem(dp + d, 4), me, lax.rem(ch + c, 2)),
                    device_id_type=MESH,
                )

    sig_t[...] = signal_ref[...].astype(F32).T
    gate_t[...] = gating_ref[...].astype(F32).T
    filt_t = filt_ref[...].T
    for cc in range(PER):
        sf_send[pl.ds(cc, n, stride=8), :] = sig_t[cc * n:(cc + 1) * n, :]
        sf_send[pl.ds(PER + cc, n, stride=8), :] = filt_t[cc * n:(cc + 1) * n, :]
    real_length = length_ref[0]
    live_col = (me * LANES + lax.broadcasted_iota(jnp.int32, (LANES, 1), 0) < real_length).astype(F32)
    live_row = (me * LANES + lax.broadcasted_iota(jnp.int32, (1, LANES), 1) < real_length).astype(F32)
    masked[...] = (cot_ref[...].astype(F32) * live_col).astype(BF)
    pick1 = index_ref[0].astype(F32)
    pick0 = 1.0 - pick1
    up_sel = (up_ref[0].astype(F32) * pick0 + up_ref[1].astype(F32) * pick1).astype(BF)
    down_sel = (down_ref[0].astype(F32) * pick0 + down_ref[1].astype(F32) * pick1).astype(BF)
    max_rank = up_sel.shape[0]
    keep = (lax.broadcasted_iota(jnp.int32, (max_rank, LANES), 0) < rank_ref[0]).astype(F32)

    pl.semaphore_wait(barrier, n - 1 + 7)

    def cot_copy(qq, hh):
        return pltpu.make_async_remote_copy(
            src_ref=cot_ref.at[:, pl.ds((2 * qq + hh) * cols, cols)],
            dst_ref=m_recv.at[dp],
            send_sem=m_send_sem.at[2 * qq + hh],
            recv_sem=m_recv_sem.at[dp],
            device_id=(2 * ch + qq, me, hh),
            device_id_type=MESH,
        )

    def cot_self(qq, hh):
        return (2 * ch + qq == dp) & (ch == hh)

    for qq in range(2):
        for hh in range(2):
            @pl.when(jnp.logical_not(cot_self(qq, hh)))
            def _():
                cot_copy(qq, hh).start()

            @pl.when(cot_self(qq, hh))
            def _():
                pltpu.make_async_copy(
                    cot_ref.at[:, pl.ds((2 * qq + hh) * cols, cols)], m_recv.at[dp], m_recv_sem.at[dp]
                ).start()

    def a2a_start(k, src, dst, size):
        def body(d, _):
            j = lax.rem(me + d, n)
            pltpu.make_async_remote_copy(
                src_ref=src.at[pl.ds(pl.multiple_of(j * size, size), size), :],
                dst_ref=dst.at[pl.ds(pl.multiple_of(me * size, size), size), :],
                send_sem=a2a_send_sem.at[k],
                recv_sem=a2a_recv_sem.at[k],
                device_id=(dp, j, ch),
                device_id_type=MESH,
            ).start()
            return 0

        lax.fori_loop(1, n, body, 0)
        mine = pl.ds(pl.multiple_of(me * size, size), size)
        pltpu.make_async_copy(src.at[mine, :], dst.at[mine, :], a2a_recv_sem.at[k]).start()

    def a2a_wait(k, dst):
        pltpu.make_async_copy(dst, dst, a2a_recv_sem.at[k]).wait()

    def a2a_wait_send(k, src, size):
        part = src.at[pl.ds(0, (n - 1) * size), :]
        pltpu.make_async_copy(part, part, a2a_send_sem.at[k]).wait()

    a2a_start(0, sf_send, sf_recv, 8)

    def to_chan(src, dst, send_sem, recv_sem):
        return pltpu.make_async_remote_copy(
            src_ref=src, dst_ref=dst, send_sem=send_sem, recv_sem=recv_sem,
            device_id=(dp, me, other), device_id_type=MESH,
        )

    w_copy = to_chan(
        w_ref.at[:, pl.ds(pl.multiple_of(other * cols, LANES), cols)], w_recv, w_sem.at[0], w_sem.at[1]
    )
    w_copy.start()
    d_send[...] = dot_t(up_sel, masked[...])
    d_copy = to_chan(d_send, d_recv, d_sem.at[0], d_sem.at[1])
    d_copy.start()

    tc, ts = tc_ref[...], ts_ref[...]

    def forward(load, store):
        x = jnp.concatenate([load(cc) for cc in range(PER)], axis=1)
        y = dot(t1_ref[...], split_data(x, 0))
        parts = []
        for cc in range(PER):
            re = y[:rows, cc * LANES:(cc + 1) * LANES]
            im = y[rows:, cc * LANES:(cc + 1) * LANES]
            parts.append(jnp.concatenate([re * tc + im * ts, im * tc - re * ts], axis=1))
        store[...] = dot(split_data(jnp.concatenate(parts, axis=0), 1), t2_ref[...])

    def inverse(re, im):
        q = dot(split_data(jnp.concatenate([re, im], axis=1), 1), t2b_ref[...])
        parts = []
        for cc in range(PER):
            qr = q[cc * rows:(cc + 1) * rows, :LANES]
            qi = q[cc * rows:(cc + 1) * rows, LANES:]
            parts.append(jnp.concatenate([qr * tc - qi * ts, qi * tc + qr * ts], axis=0))
        return dot(t1b_ref[...], split_data(jnp.concatenate(parts, axis=1), 0))

    a2a_wait(0, sf_recv)
    forward(lambda cc: sf_recv[pl.ds(cc, n, stride=8), :], spec_s)
    forward(lambda cc: sf_recv[pl.ds(PER + cc, n, stride=8), :], spec_f)
    s_re, s_im = spec_s[:, :LANES], spec_s[:, LANES:]
    f_re, f_im = spec_f[:, :LANES], spec_f[:, LANES:]
    conv = inverse(s_re * f_re - s_im * f_im, s_re * f_im + s_im * f_re)
    for cc in range(PER):
        c_send[pl.ds(cc, n, stride=HALF_ROWS), :] = conv[:, cc * LANES:(cc + 1) * LANES]
    a2a_start(1, c_send, c_recv, HALF_ROWS)

    d_copy.wait()
    back_rank = (2.0 * (d_send[...] + d_recv[...]) * keep).astype(BF)

    w_copy.wait_recv()
    order = (0, 1, 3, 2)
    own_cols = pl.ds(pl.multiple_of(ch * cols, LANES), cols)
    pre_copies, ret_copies = [], []

    def finish(slot):
        b = lax.rem(dp + order[slot], 4)
        pre_copies[slot].wait_recv()
        total = own_part[slot] + pre_recv[slot].astype(F32)
        if slot == 0:
            grady_t[...] = total
            return
        ret_send[slot] = total.astype(BF)
        copy = pltpu.make_async_remote_copy(
            src_ref=ret_send.at[slot], dst_ref=ret_recv.at[dp],
            send_sem=ret_send_sem.at[slot], recv_sem=ret_recv_sem.at[dp],
            device_id=(b, me, ch), device_id_type=MESH,
        )
        copy.start()
        ret_copies.append(copy)

    for slot in range(4):
        b = lax.rem(dp + order[slot], 4)
        pltpu.make_async_copy(m_recv.at[b], m_recv.at[b], m_recv_sem.at[b]).wait()
        piece = m_recv[b]
        pre_send[slot] = dot_t(w_recv[...], piece).astype(BF)
        copy = to_chan(pre_send.at[slot], pre_recv.at[slot], pre_send_sem.at[slot], pre_recv_sem.at[slot])
        copy.start()
        pre_copies.append(copy)
        own_part[slot] = dot_t(w_ref[:, own_cols], piece)
        if slot:
            finish(slot - 1)
    finish(3)

    skip_t = jnp.broadcast_to(skip_ref[...], (LANES, width)).T
    a2a_wait(1, c_recv)
    conv_t = jnp.concatenate(
        [c_recv[pl.ds(cc, n, stride=HALF_ROWS), :] for cc in range(PER)], axis=0
    )
    inner_t = conv_t + skip_t * sig_t[...]
    gated_t = (gate_t[...] * inner_t).astype(BF)
    r_send[...] = dot_0(down_sel, gated_t)
    r_copy = to_chan(r_send, r_recv, r_sem.at[0], r_sem.at[1])
    r_copy.start()

    total = grady_t[...]
    for step in (1, 3, 2):
        q = lax.rem(dp + step, 4)
        pltpu.make_async_copy(ret_recv.at[q], ret_recv.at[q], ret_recv_sem.at[q]).wait()
        total = total + ret_recv[q].astype(F32)
    grad_y = total * live_row + dot(down_sel, back_rank)
    grad_u = grad_y * gate_t[...]
    grady_t[...] = grad_u
    for cc in range(PER):
        u_send[pl.ds(cc, n, stride=HALF_ROWS), :] = grady_t[cc * n:(cc + 1) * n, :]
    a2a_start(2, u_send, u_recv, HALF_ROWS)
    ggat_ref[...] = (grad_y * inner_t).T.astype(BF)

    r_copy.wait()
    fwd_rank = (2.0 * (r_send[...] + r_recv[...]) * keep).astype(BF)
    b_send[:, :half] = dot(fwd_rank, masked[...]).astype(BF)
    b_send[:, half:half + width] = dot_t(back_rank, gated_t).astype(BF)
    product = grad_u * sig_t[...]
    high = product.astype(BF)
    low = (product - high.astype(F32)).astype(BF)
    ones = jnp.ones((max_rank, LANES), BF)
    b_send[:, half + a_chunks * LANES:half + a_chunks * LANES + width] = (
        dot_t(ones, high) + dot_t(ones, low)
    ).astype(BF)

    def share(d, _):
        p = lax.rem(me + d, n_own)
        src = b_send.at[:, pl.ds(pl.multiple_of(p * LANES, LANES), LANES)]
        dst = b_recv.at[pl.ds(pl.multiple_of(me * 16, 16), 16), :]

        @pl.when(p != me)
        def _():
            pltpu.make_async_remote_copy(
                src_ref=src, dst_ref=dst, send_sem=b_sem.at[0], recv_sem=b_sem.at[1],
                device_id=(dp, p, ch), device_id_type=MESH,
            ).start()

        @pl.when(p == me)
        def _():
            pltpu.make_async_copy(src, dst, b_sem.at[1]).start()
        return 0

    lax.fori_loop(0, n_own, share, 0)

    a2a_wait(2, u_recv)
    forward(lambda cc: u_recv[pl.ds(cc, n, stride=HALF_ROWS), :], spec_g)
    g_re, g_im = spec_g[:, :LANES], spec_g[:, LANES:]
    s_re, s_im = spec_s[:, :LANES], spec_s[:, LANES:]
    f_re, f_im = spec_f[:, :LANES], spec_f[:, LANES:]
    corr_f = inverse(g_re * f_re + g_im * f_im, g_im * f_re - g_re * f_im)
    corr_s = inverse(g_re * s_re + g_im * s_im, g_im * s_re - g_re * s_im)
    for cc in range(PER):
        k_send[pl.ds(cc, n, stride=8), :] = corr_f[:, cc * LANES:(cc + 1) * LANES]
        k_send[pl.ds(PER + cc, n, stride=8), :] = corr_s[:, cc * LANES:(cc + 1) * LANES]
    a2a_start(3, k_send, k_recv, 8)

    is_owner = me < n_own

    def q_copy(step):
        return pltpu.make_async_remote_copy(
            src_ref=q_send, dst_ref=q_recv.at[dp], send_sem=q_send_sem.at[step], recv_sem=q_recv_sem.at[dp],
            device_id=(lax.rem(dp + step, 4), me, ch), device_id_type=MESH,
        )

    @pl.when(is_owner)
    def _():
        pltpu.make_async_copy(b_recv, b_recv, b_sem.at[1]).wait()
        acc = b_recv[0:16, :].astype(F32)
        for i in range(1, n):
            acc = acc + b_recv[16 * i:16 * (i + 1), :].astype(F32)
        q_send[...] = jnp.concatenate([acc * pick0, acc * pick1], axis=0)
        for step in (1, 3, 2):
            q_copy(step).start()

    a2a_wait(3, k_recv)
    corr_st = jnp.concatenate(
        [k_recv[pl.ds(PER + cc, n, stride=8), :] for cc in range(PER)], axis=0
    )
    f_send[...] = corr_st.astype(BF)
    f_copies = []
    for step in (1, 3, 2):
        copy = pltpu.make_async_remote_copy(
            src_ref=f_send, dst_ref=f_recv.at[dp], send_sem=f_send_sem.at[step], recv_sem=f_recv_sem.at[dp],
            device_id=(lax.rem(dp + step, 4), me, ch), device_id_type=MESH,
        )
        copy.start()
        f_copies.append(copy)

    g_size = 2 * max_rank

    @pl.when(is_owner)
    def _():
        sums = q_send[...]
        for step in (1, 3, 2):
            q = lax.rem(dp + step, 4)
            pltpu.make_async_copy(q_recv.at[q], q_recv.at[q], q_recv_sem.at[q]).wait()
            sums = sums + q_recv[q]
        g_send[...] = sums.astype(BF)
        mine = pl.ds(pl.multiple_of(me * g_size, g_size), g_size)

        def spread(d, _):
            pltpu.make_async_remote_copy(
                src_ref=g_send, dst_ref=g_recv.at[mine, :], send_sem=g_sem.at[0], recv_sem=g_sem.at[1],
                device_id=(dp, lax.rem(me + d, n), ch), device_id_type=MESH,
            ).start()
            return 0

        lax.fori_loop(1, n, spread, 0)
        pltpu.make_async_copy(g_send, g_recv.at[mine, :], g_sem.at[1]).start()

    corr_ft = jnp.concatenate(
        [k_recv[pl.ds(cc, n, stride=8), :] for cc in range(PER)], axis=0
    )
    gsig_ref[...] = (corr_ft + skip_t * grady_t[...]).T.astype(BF)

    sums = corr_st
    for step in (1, 3, 2):
        q = lax.rem(dp + step, 4)
        pltpu.make_async_copy(f_recv.at[q], f_recv.at[q], f_recv_sem.at[q]).wait()
        sums = sums + f_recv[q].astype(F32)
    gfilt_ref[...] = sums.T

    pltpu.make_async_copy(g_recv, g_recv, g_sem.at[1]).wait()

    def place(p, _):
        block = g_recv[pl.ds(pl.multiple_of(p * g_size, g_size), g_size), :].astype(F32)
        where = pl.ds(pl.multiple_of(p * LANES, LANES), LANES)
        gb_ref[0, :, where] = block[:max_rank]
        gb_ref[1, :, where] = block[max_rank:]
        return 0

    lax.fori_loop(0, up_chunks, place, 0)
    for k in range(a_chunks):
        size = min(LANES, width)
        at = (up_chunks + k) * g_size
        block = g_recv[at:at + g_size, :].astype(F32)
        ga_ref[0, :, k * size:(k + 1) * size] = block[:max_rank, :size]
        ga_ref[1, :, k * size:(k + 1) * size] = block[max_rank:, :size]
        at = (up_chunks + a_chunks + k) * g_size
        block = g_recv[at:at + g_size, :].astype(F32)
        gskip_ref[:, k * size:(k + 1) * size] = (block[:max_rank] + block[max_rank:])[:8, :size]

    for qq in range(2):
        for hh in range(2):
            @pl.when(jnp.logical_not(cot_self(qq, hh)))
            def _():
                cot_copy(qq, hh).wait_send()
    a2a_wait_send(0, sf_send, 8)
    a2a_wait_send(1, c_send, HALF_ROWS)
    a2a_wait_send(2, u_send, HALF_ROWS)
    a2a_wait_send(3, k_send, 8)
    w_copy.wait_send()
    for copy in pre_copies + ret_copies + f_copies:
        copy.wait_send()

    def b_sent(count):
        part = b_send.at[:, pl.ds(0, count * LANES)]
        pltpu.make_async_copy(part, part, b_sem.at[0]).wait()

    @pl.when(is_owner)
    def _():
        b_sent(n_own - 1)
        for step in (1, 3, 2):
            q_copy(step).wait_send()

        def sent(d, _):
            pltpu.make_async_copy(g_send, g_send, g_sem.at[0]).wait()
            return 0

        lax.fori_loop(1, n, sent, 0)

    @pl.when(jnp.logical_not(is_owner))
    def _():
        b_sent(n_own)


def local(
    signal, gating, cotangent, filt, skip, output_projection,
    adapter_down_bank, adapter_up_bank, adapter_index, sequence_rank, real_length,
):
    n = lax.axis_size("seq")
    width = signal.shape[2]
    half = cotangent.shape[2]
    cols = output_projection.shape[1] // 2
    max_rank = adapter_up_bank.shape[1]
    a_chunks = -(-width // LANES)
    n_own = half // LANES + 2 * a_chunks
    consts = [jnp.asarray(t) for t in tables(n)]
    rows = consts[4].shape[0]
    vmem = pl.BlockSpec(memory_space=pltpu.VMEM)
    smem = pl.BlockSpec(memory_space=pltpu.SMEM)
    dma = pltpu.SemaphoreType.DMA
    outs = pl.pallas_call(
        functools.partial(kernel, n),
        out_shape=(
            jax.ShapeDtypeStruct((LANES, width), BF),
            jax.ShapeDtypeStruct((LANES, width), BF),
            jax.ShapeDtypeStruct((LANES, width), F32),
            jax.ShapeDtypeStruct((8, width), F32),
            jax.ShapeDtypeStruct((2, max_rank, width), F32),
            jax.ShapeDtypeStruct((2, max_rank, half), F32),
        ),
        in_specs=[smem] * 3 + [vmem] * 14,
        out_specs=(vmem,) * 6,
        scratch_shapes=[
            pltpu.VMEM((LANES, half), BF),
            pltpu.VMEM((width, LANES), F32),
            pltpu.VMEM((width, LANES), F32),
            pltpu.VMEM((width, LANES), F32),
            pltpu.VMEM((PER * rows, 2 * LANES), F32),
            pltpu.VMEM((PER * rows, 2 * LANES), F32),
            pltpu.VMEM((PER * rows, 2 * LANES), F32),
            pltpu.VMEM((8 * n, LANES), F32),
            pltpu.VMEM((8 * n, LANES), F32),
            pltpu.VMEM((HALF_ROWS * n, LANES), F32),
            pltpu.VMEM((HALF_ROWS * n, LANES), F32),
            pltpu.VMEM((HALF_ROWS * n, LANES), F32),
            pltpu.VMEM((HALF_ROWS * n, LANES), F32),
            pltpu.VMEM((8 * n, LANES), F32),
            pltpu.VMEM((8 * n, LANES), F32),
            pltpu.VMEM((4, LANES, cols), BF),
            pltpu.VMEM((width, cols), BF),
            pltpu.VMEM((4, width, LANES), BF),
            pltpu.VMEM((4, width, LANES), BF),
            pltpu.VMEM((4, width, LANES), F32),
            pltpu.VMEM((4, width, LANES), BF),
            pltpu.VMEM((4, width, LANES), BF),
            pltpu.VMEM((max_rank, LANES), F32),
            pltpu.VMEM((max_rank, LANES), F32),
            pltpu.VMEM((max_rank, LANES), F32),
            pltpu.VMEM((max_rank, LANES), F32),
            pltpu.VMEM((max_rank, n_own * LANES), BF),
            pltpu.VMEM((16 * n, LANES), BF),
            pltpu.VMEM((2 * max_rank, LANES), F32),
            pltpu.VMEM((4, 2 * max_rank, LANES), F32),
            pltpu.VMEM((2 * max_rank, LANES), BF),
            pltpu.VMEM((2 * max_rank * n_own, LANES), BF),
            pltpu.VMEM((width, LANES), BF),
            pltpu.VMEM((4, width, LANES), BF),
            dma((4,)), dma((4,)), dma((4,)), dma((4,)), dma((2,)), dma((4,)), dma((4,)),
            dma((4,)), dma((4,)), dma((2,)), dma((2,)), dma((2,)), dma((4,)), dma((4,)), dma((2,)),
            dma((4,)), dma((4,)),
        ],
        compiler_params=pltpu.CompilerParams(
            collective_id=0, has_side_effects=True, vmem_limit_bytes=40 * 1024 * 1024
        ),
    )(
        adapter_index, sequence_rank, real_length,
        signal[0], gating[0], cotangent[0], filt, skip[None], output_projection,
        adapter_down_bank, adapter_up_bank, *consts,
    )
    grad_signal, grad_gating, grad_filt, grad_skip, grad_a, grad_b = outs
    return (
        grad_signal[None], grad_gating[None], grad_filt, grad_skip[0],
        jnp.swapaxes(grad_a, 1, 2), grad_b,
    )


def solution(mesh):
    placed = (
        P("dp", "seq", "chan"), P("dp", "seq", "chan"), P("dp", "seq", "chan"), P("seq", "chan"),
        P("chan"), P("chan", "dp"), P(None, "chan", None), P(None, None, "chan"),
        P("dp"), P("dp"), P("dp"),
    )
    return jax.shard_map(
        local,
        mesh=mesh,
        in_specs=placed,
        out_specs=(
            P("dp", "seq", "chan"), P("dp", "seq", "chan"), P("seq", "chan"), P("chan"),
            P(None, "chan", None), P(None, None, "chan"),
        ),
        check_vma=False,
    )
```

time: 1800 us -> 113 us (0.06)
  blocking collectives: 1370 us -> 0 us
  waiting for transfers between devices: 221 us -> 0 us
  starting transfers between devices: 114 us -> 0 us
  Pallas kernels: 0 us -> 94 us
  matrix products: 31.1 us -> 0 us
    psum x2 -> x0, blocking collectives: 1360 us -> none  [the longest x1 1360 us: local(): lax.psum((a_bank, b_bank, skip_term), ('dp', 'seq'))]
    all_to_all x17 -> x0, waiting for transfers between devices: 162 us -> none  [the longest x1 21.7 us: local(): lax.all_to_all(partials[0], 'seq', split_axis=1, concat_axis=0, tiled=True)]
    all_to_all x17 -> x0, starting transfers between devices: 114 us -> none  [the longest x1 14.4 us: local(): lax.all_to_all(partials[0], 'seq', split_axis=1, concat_axis=0, tiled=True)]
    pallas_call x0 -> x1, Pallas kernels: none -> 94 us  [local(): pl.pallas_call(functools.partial(kernel, n), out_shape=(jax.ShapeDtypeStr...]
    psum x2 -> x0, waiting for transfers between devices: 59.1 us -> none  [the longest x1 59.1 us: local(): grad_filt = lax.psum(corr_signal, 'dp')]
    dot_general x44 -> x0, matrix products: 31.1 us -> none  [the longest x24 16.6 us: apply_table(): return jnp.einsum('jn,knc->kjc', table, values, precision=HIGHEST_PRECISION)]
  transfers between devices with their start and end apart: 21 -> 0, of which waited for: 17 -> 0; matrix products, arithmetic and copies ran while one was open for 2% -> 0% of each run, Pallas kernels for 0% -> 0%
where the time goes in v1:
time: 113 us; the launch traced here: 112 us
  Pallas kernels  94 us (83%)
  local copies, waits for them, and re-layouts  15 us (13%)
  between operations  2.67 us (2%)
    pallas_call x1, Pallas kernels, local(): pl.pallas_call(functools.partial(kernel, n), out_shape=(jax.ShapeDtypeStr...  94 us
    unnamed x32, local copies, waits for them, and re-layouts  14.4 us

profile of v1, /device:TPU:6, one launch (start us, length us, event | category | flops | bytes accessed | tf_op | source)
XLA Modules:
  0.0 111.6 jit_solution(60632632099834732)
XLA Ops:
  0.6 0.0 copy-start.10
  0.6 0.0 copy-start.5
  2.6 0.8 copy.23.down_ref
  3.5 0.0 copy-done.10
  3.5 0.0 copy-done.5
  3.5 0.0 copy-start
  3.5 1.2 %copy-done = bf16[1,128,4096]{2,1,0:T(8,128)(2,1)S(1)} copy-done((bf16[1,128,4096]{2,1,0:T(8,128)(2,1)S(1)}, bf16[1,128,4096]{2,1,0:T(8,128)(2,1)}, u32[]{:S(2)}) %copy-start) | copy-done | bytes 1048600
  4.7 0.0 copy-start.1
  4.7 1.2 %copy-done.1 = bf16[256,2048]{1,0:T(8,128)(2,1)S(1)} copy-done((bf16[256,2048]{1,0:T(8,128)(2,1)S(1)}, bf16[256,2048]{1,0:T(8,128)(2,1)}, u32[]{:S(2)}) %copy-start.1) | copy-done | bytes 1048600
  5.9 0.0 copy-start.2
  5.9 1.0 copy-done.2
  6.9 0.0 copy-start.3
  6.9 1.0 copy-done.3
  7.9 0.0 copy-start.4
  7.9 0.9 copy-done.4
  8.9 0.0 copy-start.6
  8.9 0.9 copy-done.6
  9.8 0.0 copy-start.7
  9.8 0.8 copy-done.7
  10.6 0.0 copy-start.8
  10.6 0.8 copy-done.8
  11.4 0.0 copy-start.9
  11.5 0.8 copy-done.9
  12.3 0.8 copy-done.11
  13.1 0.7 copy-done.12
  13.7 94.0 %shard_map.208 = (bf16[128,256]{1,0:T(8,128)(2,1)S(1)}, bf16[128,256]{1,0:T(8,128)(2,1)S(1)}, f32[128,256]{1,0:T(8,128)S(1)}, f32[8,256]{1,0:T(8,128)S(1)}, f32[...) custom-call(s32[1]{0:T(128)S(6)} %copy.29.index_ref, s32[1]{0:T(128)S(6)} %copy.30.rank_ref, s32[1]{0:T(128)S(6)} %copy.31.length_ref, ...), custom_call_target="tpu_custom_call" | custom-call | tf_op jit(solution)/shard_map/pallas_call | solution.py:471
  107.8 0.6 slice.3
  108.3 0.6 copy.32
  109.0 0.6 copy.33
  109.6 0.7 copy.34
  110.2 0.6 copy.35
  110.9 0.8 copy.36
  (2 shorter events, 0.0 us)
Async XLA Ops:
  0.6 2.8 %copy-start.10 = (f32[72,128]{1,0:T(8,128)S(1)}, f32[72,128]{1,0:T(8,128)}, u32[]{:S(2)}) copy-start(f32[72,128]{1,0:T(8,128)} %constant.17.clone.ts_ref) | copy-start | bytes 110596
  0.6 2.8 %copy-start.5 = (f32[128,256]{1,0:T(8,128)S(1)}, f32[128,256]{1,0:T(8,128)}, u32[]{:S(2)}) copy-start(f32[128,256]{1,0:T(8,128)} %filt_ref.1) | copy-start | bytes 393220
  3.5 1.2 %copy-start = (bf16[1,128,4096]{2,1,0:T(8,128)(2,1)S(1)}, bf16[1,128,4096]{2,1,0:T(8,128)(2,1)}, u32[]{:S(2)}) copy-start(bf16[1,128,4096]{2,1,0:T(8,128)(2,1)} %param.19) | copy-start | bytes 3145732
  4.7 1.2 %copy-start.1 = (bf16[256,2048]{1,0:T(8,128)(2,1)S(1)}, bf16[256,2048]{1,0:T(8,128)(2,1)}, u32[]{:S(2)}) copy-start(bf16[256,2048]{1,0:T(8,128)(2,1)} %w_ref.1) | copy-start | bytes 3145732
  5.9 1.0 copy-start.2
  6.9 1.0 copy-start.3
  7.9 0.9 copy-start.4
  8.9 0.9 copy-start.6
  9.8 0.8 copy-start.7
  10.6 0.8 copy-start.8
  11.4 0.8 copy-start.9
  12.3 0.8 copy-start.11
  13.1 0.7 copy-start.12

commit v2 on v1

v2 whole, which is shorter than its diff:
```python
import functools
import math

import jax
import jax.numpy as jnp
import ml_dtypes
import numpy as np
from jax import lax
from jax.experimental import pallas as pl
from jax.experimental.pallas import tpu as pltpu
from jax.sharding import PartitionSpec as P

MESH = pl.DeviceIdType.MESH
BF = jnp.bfloat16
F32 = jnp.float32
LANES = 128
PER = 4
VMEM_LIMIT = 62 * 1024 * 1024
SUB = 2


def split3(table, axis, order):
    high = table.astype(ml_dtypes.bfloat16)
    low = (table - high.astype(np.float64)).astype(ml_dtypes.bfloat16)
    return np.concatenate([high if o else low for o in order], axis=axis)


def tables(n):
    rows = -(-(n + 1) // 8) * 8
    k1 = np.arange(rows)
    used = (k1 <= n).astype(np.float64)
    i = np.arange(n)
    a = np.arange(LANES)
    period = 2 * n * LANES
    th1 = 2 * math.pi * (k1[:, None] * i[None, :] % (2 * n)) / (2 * n)
    first = np.concatenate([np.cos(th1) * used[:, None], -np.sin(th1) * used[:, None]], 0)
    thw = 2 * math.pi * (k1[:, None] * a[None, :] % period) / period
    tw_cos, tw_sin = np.cos(thw), np.sin(thw)
    th2 = 2 * math.pi * (a[:, None] * a[None, :] % LANES) / LANES
    c2, s2 = np.cos(th2), np.sin(th2)
    second = np.block([[c2, -s2], [s2, c2]])
    second_back = np.block([[c2, s2], [-s2, c2]])
    weight = used * np.where((k1 == 0) | (k1 == n), 1.0, 2.0) / period
    last = np.concatenate([np.cos(th1).T * weight, -np.sin(th1).T * weight], 1)
    return (
        split3(first, 1, (1, 1, 0)),
        split3(second, 0, (1, 1, 0)),
        split3(second_back, 0, (1, 1, 0)),
        split3(last, 1, (1, 1, 0)),
        tw_cos.astype(np.float32),
        tw_sin.astype(np.float32),
    )


def split_data(x, axis):
    high = x.astype(BF)
    low = (x - high.astype(F32)).astype(BF)
    return jnp.concatenate([high, low, high], axis=axis)


def dot(a, b):
    return jnp.dot(a, b, preferred_element_type=F32)


def dot_t(a, b):
    return lax.dot_general(a, b, (((1,), (1,)), ((), ())), preferred_element_type=F32)


def dot_0(a, b):
    return lax.dot_general(a, b, (((0,), (0,)), ((), ())), preferred_element_type=F32)


def kernel(
    n,
    index_ref, rank_ref, length_ref,
    signal_hbm, gating_hbm, cot_hbm, filt_hbm, skip_hbm, w_hbm, down_hbm, up_hbm,
    t1_hbm, t2_hbm, t2b_hbm, t1b_hbm, tc_hbm, ts_hbm,
    gsig_hbm, ggat_hbm, gfilt_hbm, gbank_hbm, gskip_hbm,
    gsig_ref, ggat_ref, gfilt_ref, gskip_ref,
    signal_ref, gating_ref, cot_ref, filt_ref, skip_ref, w_ref, down_ref, up_ref,
    t1_ref, t2_ref, t2b_ref, t1b_ref, tc_ref, ts_ref,
    masked, sig_t, gate_t, gradu_t, spec_s, spec_f, spec_g,
    sf_send, sf_recv, c_send, c_recv, u_send, u_recv, ks_send, ks_recv, kf_send, kf_recv,
    m_own, m_recv, w_recv, pre0_send, pre0_recv, pre_send, pre_recv, ret_send, ret_recv,
    d_send, d_recv, r_send, r_recv,
    b_send, b_recv, q_send, q_recv, g_send, g_recv, f_send, f_recv, e_send, e_recv,
    in_sem, out_sem, a2a_send_sem, a2a_recv_sem, m_send_sem, m_recv_sem, own_sem, w_sem, pre0_sem,
    pre_send_sem, pre_recv_sem, ret_send_sem, ret_recv_sem, d_sem, r_sem, b_sem,
    q_send_sem, q_recv_sem, g_sem, f_send_sem, f_recv_sem, e_send_sem, e_recv_sem,
):
    dp = lax.axis_index("dp")
    me = lax.axis_index("seq")
    ch = lax.axis_index("chan")
    other = 1 - ch
    plane = n // 2
    zl, spot = lax.div(me, plane), lax.rem(me, plane)
    width = w_ref.shape[0]
    cols = w_ref.shape[1] // 2
    half = cot_ref.shape[1]
    piece = LANES // SUB
    n_own = b_send.shape[1] // LANES
    rows = t1_ref.shape[0] // 2
    a_chunks = -(-width // LANES)

    barrier = pltpu.get_barrier_semaphore()
    for d in range(4):
        for z in range(2):
            for c in range(2):
                if d or c:
                    pl.semaphore_signal(
                        barrier, inc=1,
                        device_id=(lax.rem(dp + d, 4), lax.rem(zl + z, 2) * plane + spot, lax.rem(ch + c, 2)),
                        device_id_type=MESH,
                    )

    def greet(d, _):
        pl.semaphore_signal(
            barrier, inc=1, device_id=(dp, lax.rem(me + d, n), ch), device_id_type=MESH
        )
        return 0

    lax.fori_loop(1, n, greet, 0, unroll=9 if n == 64 else 1)

    pairs = (
        (signal_hbm, signal_ref), (filt_hbm, filt_ref), (cot_hbm, cot_ref), (up_hbm, up_ref),
        (w_hbm, w_ref), (t1_hbm, t1_ref), (t2_hbm, t2_ref), (t2b_hbm, t2b_ref), (t1b_hbm, t1b_ref),
        (tc_hbm, tc_ref), (ts_hbm, ts_ref), (gating_hbm, gating_ref), (down_hbm, down_ref),
        (skip_hbm, skip_ref),
    )
    loads = [pltpu.make_async_copy(s, d, in_sem.at[i]) for i, (s, d) in enumerate(pairs)]
    for load in loads:
        load.start()

    loads[0].wait()
    loads[1].wait()
    sig_t[...] = signal_ref[...].astype(F32).T
    filt_t = filt_ref[...].T
    for cc in range(PER):
        sf_send[pl.ds(cc, n, stride=8), :] = sig_t[cc * n:(cc + 1) * n, :]
        sf_send[pl.ds(PER + cc, n, stride=8), :] = filt_t[cc * n:(cc + 1) * n, :]
    real_length = length_ref[0]
    live_col = (me * LANES + lax.broadcasted_iota(jnp.int32, (LANES, 1), 0) < real_length).astype(F32)
    live_row = (me * LANES + lax.broadcasted_iota(jnp.int32, (1, LANES), 1) < real_length).astype(F32)
    pick1 = index_ref[0].astype(F32)
    pick0 = 1.0 - pick1

    pl.semaphore_wait(barrier, n - 1 + 14)

    def cot_copy(sub, qq, hh):
        q = 2 * ch + qq
        step = lax.rem(q - dp + 4, 4)
        odd = lax.rem(step, 2)
        to_z = lax.div(step, 3) + (1 - odd) * (1 - zl)
        return pltpu.make_async_remote_copy(
            src_ref=cot_hbm.at[pl.ds(sub * piece, piece), pl.ds((2 * qq + hh) * cols, cols)],
            dst_ref=m_recv.at[sub, odd * zl + (1 - odd) * 2],
            send_sem=m_send_sem.at[sub, 2 * qq + hh],
            recv_sem=m_recv_sem.at[sub],
            device_id=(q, to_z * plane + spot, hh),
            device_id_type=MESH,
        )

    def own_copy(qq, hh):
        return pltpu.make_async_remote_copy(
            src_ref=cot_hbm.at[:, pl.ds((2 * qq + hh) * cols, cols)],
            dst_ref=m_own,
            send_sem=own_sem.at[0],
            recv_sem=own_sem.at[1],
            device_id=(dp, me, hh),
            device_id_type=MESH,
        )

    def to_other(qq):
        return 2 * ch + qq != dp

    for sub in range(SUB):
        for qq in range(2):
            for hh in range(2):
                @pl.when(to_other(qq))
                def _():
                    cot_copy(sub, qq, hh).start()
    for qq in range(2):
        for hh in range(2):
            @pl.when((2 * ch + qq == dp) & (ch != hh))
            def _():
                own_copy(qq, hh).start()

            @pl.when((2 * ch + qq == dp) & (ch == hh))
            def _():
                pltpu.make_async_copy(
                    cot_hbm.at[:, pl.ds((2 * qq + hh) * cols, cols)], m_own, own_sem.at[1]
                ).start()

    def to_chan(src, dst, send_sem, recv_sem):
        return pltpu.make_async_remote_copy(
            src_ref=src, dst_ref=dst, send_sem=send_sem, recv_sem=recv_sem,
            device_id=(dp, me, other), device_id_type=MESH,
        )

    w_copy = to_chan(
        w_hbm.at[:, pl.ds(pl.multiple_of(other * cols, LANES), cols)], w_recv, w_sem.at[0], w_sem.at[1]
    )
    w_copy.start()

    def a2a_start(k, src, dst, at):
        def body(d, _):
            j = lax.rem(me + d, n)
            pltpu.make_async_remote_copy(
                src_ref=src.at[at(j)],
                dst_ref=dst.at[at(me)],
                send_sem=a2a_send_sem.at[k],
                recv_sem=a2a_recv_sem.at[k],
                device_id=(dp, j, ch),
                device_id_type=MESH,
            ).start()
            return 0

        lax.fori_loop(1, n, body, 0, unroll=9 if n == 64 else 1)
        pltpu.make_async_copy(src.at[at(me)], dst.at[at(me)], a2a_recv_sem.at[k]).start()

    def a2a_wait(k, dst):
        pltpu.make_async_copy(dst, dst, a2a_recv_sem.at[k]).wait()

    def a2a_wait_send(k, src, size):
        part = src.at[pl.ds(0, (n - 1) * size)]
        pltpu.make_async_copy(part, part, a2a_send_sem.at[k]).wait()

    def eight(j):
        return pl.ds(pl.multiple_of(j * 8, 8), 8)

    def block(j):
        return j

    a2a_start(0, sf_send, sf_recv, eight)

    for load in loads[2:]:
        load.wait()
    masked[...] = (cot_ref[...].astype(F32) * live_col).astype(BF)
    up_sel = (up_ref[0].astype(F32) * pick0 + up_ref[1].astype(F32) * pick1).astype(BF)
    down_sel = (down_ref[0].astype(F32) * pick0 + down_ref[1].astype(F32) * pick1).astype(BF)
    max_rank = up_sel.shape[0]
    keep = (lax.broadcasted_iota(jnp.int32, (max_rank, LANES), 0) < rank_ref[0]).astype(F32)
    d_send[...] = dot_t(up_sel, masked[...])
    d_copy = to_chan(d_send, d_recv, d_sem.at[0], d_sem.at[1])
    d_copy.start()
    gate_t[...] = gating_ref[...].astype(F32).T
    skip_t = jnp.broadcast_to(skip_ref[...], (LANES, width)).T

    own_cols = pl.ds(pl.multiple_of(ch * cols, LANES), cols)
    pltpu.make_async_copy(m_own, m_own, own_sem.at[1]).wait()
    w_copy.wait_recv()
    pre0_send[...] = dot_t(m_own[...], w_recv[...]).astype(BF)
    pre0_copy = to_chan(pre0_send, pre0_recv, pre0_sem.at[0], pre0_sem.at[1])
    pre0_copy.start()
    own_part = dot_t(m_own[...], w_ref[:, own_cols])

    pre_copies, ret_copies = [], []

    def project(sub):
        pltpu.make_async_copy(m_recv.at[sub], m_recv.at[sub], m_recv_sem.at[sub]).wait()
        part = m_recv[sub].reshape(3 * piece, cols)
        pre_send[sub] = dot_t(part, w_recv[...]).astype(BF)
        copy = to_chan(pre_send.at[sub], pre_recv.at[sub], pre_send_sem.at[sub], pre_recv_sem.at[sub])
        copy.start()
        pre_copies.append(copy)
        return dot_t(part, w_ref[:, own_cols])

    def give_back(sub, mine):
        pre_copies[sub].wait_recv()
        ret_send[sub] = (mine + pre_recv[sub].astype(F32)).astype(BF)
        near, far = lax.rem(dp + 3 - 2 * zl, 4), lax.rem(dp + 2, 4)
        for slot, (b, z, back) in enumerate(((near, 0, zl), (near, 1, zl), (far, 1 - zl, 2))):
            copy = pltpu.make_async_remote_copy(
                src_ref=ret_send.at[sub, pl.ds(slot * piece, piece)],
                dst_ref=ret_recv.at[back, pl.ds(sub * piece, piece)],
                send_sem=ret_send_sem.at[sub, slot], recv_sem=ret_recv_sem,
                device_id=(b, z * plane + spot, ch), device_id_type=MESH,
            )
            copy.start()
            ret_copies.append(copy)

    tc, ts = tc_ref[...], ts_ref[...]

    def forward(load, store):
        x = jnp.concatenate([load(cc) for cc in range(PER)], axis=1)
        y = dot(t1_ref[...], split_data(x, 0))
        parts = []
        for cc in range(PER):
            re = y[:rows, cc * LANES:(cc + 1) * LANES]
            im = y[rows:, cc * LANES:(cc + 1) * LANES]
            parts.append(jnp.concatenate([re * tc + im * ts, im * tc - re * ts], axis=1))
        store[...] = dot(split_data(jnp.concatenate(parts, axis=0), 1), t2_ref[...])

    def inverse(re, im):
        q = dot(split_data(jnp.concatenate([re, im], axis=1), 1), t2b_ref[...])
        parts = []
        for cc in range(PER):
            qr = q[cc * rows:(cc + 1) * rows, :LANES]
            qi = q[cc * rows:(cc + 1) * rows, LANES:]
            parts.append(jnp.concatenate([qr * tc - qi * ts, qi * tc + qr * ts], axis=0))
        return dot(t1b_ref[...], split_data(jnp.concatenate(parts, axis=1), 0))

    def spread_channels(dst, values):
        for cc in range(PER):
            dst[:, cc, :] = values[:, cc * LANES:(cc + 1) * LANES]

    def gather_channels(src):
        return jnp.concatenate([src[:, cc, :] for cc in range(PER)], axis=0)

    a2a_wait(0, sf_recv)
    forward(lambda cc: sf_recv[pl.ds(cc, n, stride=8), :], spec_s)
    forward(lambda cc: sf_recv[pl.ds(PER + cc, n, stride=8), :], spec_f)
    s_re, s_im = spec_s[:, :LANES], spec_s[:, LANES:]
    f_re, f_im = spec_f[:, :LANES], spec_f[:, LANES:]
    spread_channels(c_send, inverse(s_re * f_re - s_im * f_im, s_re * f_im + s_im * f_re))
    a2a_start(1, c_send, c_recv, block)

    d_copy.wait()
    back_rank = (2.0 * (d_send[...] + d_recv[...]) * keep).astype(BF)

    a2a_wait(1, c_recv)
    inner_t = gather_channels(c_recv) + skip_t * sig_t[...]
    gated_t = (gate_t[...] * inner_t).astype(BF)
    r_send[...] = dot(down_sel, gated_t)
    r_copy = to_chan(r_send, r_recv, r_sem.at[0], r_sem.at[1])
    r_copy.start()
    b_send[:, half:half + width] = dot_t(back_rank, gated_t).astype(BF)

    r_copy.wait()
    fwd_rank = (2.0 * (r_send[...] + r_recv[...]) * keep).astype(BF)
    b_send[:, :half] = dot(fwd_rank, masked[...]).astype(BF)

    def share_copy(p):
        return pltpu.make_async_remote_copy(
            src_ref=b_send.at[:, pl.ds(pl.multiple_of(p * LANES, LANES), LANES)],
            dst_ref=b_recv.at[pl.ds(pl.multiple_of(me * 16, 16), 16), :],
            send_sem=b_sem.at[0], recv_sem=b_sem.at[1], device_id=(dp, p, ch), device_id_type=MESH,
        )

    def share(d, _):
        p = lax.rem(me + d, n_own)

        @pl.when(p != me)
        def _():
            share_copy(p).start()

        @pl.when(p == me)
        def _():
            pltpu.make_async_copy(
                b_send.at[:, pl.ds(pl.multiple_of(p * LANES, LANES), LANES)],
                b_recv.at[pl.ds(pl.multiple_of(me * 16, 16), 16), :],
                b_sem.at[1],
            ).start()
        return 0

    lax.fori_loop(0, n_own, share, 0)

    mine = project(0)
    for sub in range(1, SUB):
        after = project(sub)
        give_back(sub - 1, mine)
        mine = after
    give_back(SUB - 1, mine)

    is_owner = me < n_own

    def q_copy(step):
        return pltpu.make_async_remote_copy(
            src_ref=q_send, dst_ref=q_recv.at[step - 1], send_sem=q_send_sem.at[step],
            recv_sem=q_recv_sem, device_id=(lax.rem(dp + step, 4), me, ch), device_id_type=MESH,
        )

    @pl.when(is_owner)
    def _():
        pltpu.make_async_copy(b_recv, b_recv, b_sem.at[1]).wait()
        acc = b_recv[0:16, :].astype(F32)
        for i in range(1, n):
            acc = acc + b_recv[16 * i:16 * (i + 1), :].astype(F32)
        q_send[...] = jnp.concatenate([acc * pick0, acc * pick1], axis=0)
        for step in (1, 3, 2):
            q_copy(step).start()

    grad_y = own_part + received(pre0_copy, pre0_recv)
    pltpu.make_async_copy(ret_recv, ret_recv, ret_recv_sem).wait()
    for k in range(3):
        grad_y = grad_y + ret_recv[k].astype(F32)
    grad_y = grad_y.T * live_row + dot_0(down_sel, back_rank)
    grad_u = grad_y * gate_t[...]
    gradu_t[...] = grad_u
    for cc in range(PER):
        u_send[:, cc, :] = gradu_t[cc * n:(cc + 1) * n, :]
    a2a_start(2, u_send, u_recv, block)
    ggat_ref[...] = (grad_y * inner_t).T.astype(BF)
    outs = [
        pltpu.make_async_copy(s, d, out_sem.at[i])
        for i, (s, d) in enumerate((
            (ggat_ref, ggat_hbm), (gsig_ref, gsig_hbm), (gfilt_ref, gfilt_hbm), (g_recv, gbank_hbm),
            (gskip_ref, gskip_hbm),
        ))
    ]
    outs[0].start()

    g_size = 2 * max_rank

    @pl.when(is_owner)
    def _():
        pltpu.make_async_copy(q_recv, q_recv, q_recv_sem).wait()
        g_send[...] = (q_send[...] + q_recv[0] + q_recv[1] + q_recv[2]).astype(BF)
        at = pl.ds(pl.multiple_of(me * g_size, g_size), g_size)

        def spread(d, _):
            pltpu.make_async_remote_copy(
                src_ref=g_send, dst_ref=g_recv.at[at, :], send_sem=g_sem.at[0], recv_sem=g_sem.at[1],
                device_id=(dp, lax.rem(me + d, n), ch), device_id_type=MESH,
            ).start()
            return 0

        lax.fori_loop(1, n, spread, 0, unroll=9 if n == 64 else 1)
        pltpu.make_async_copy(g_send, g_recv.at[at, :], g_sem.at[1]).start()

    a2a_wait(2, u_recv)
    forward(lambda cc: u_recv[:, cc, :], spec_g)
    g_re, g_im = spec_g[:, :LANES], spec_g[:, LANES:]
    s_re, s_im = spec_s[:, :LANES], spec_s[:, LANES:]
    spread_channels(ks_send, inverse(g_re * s_re + g_im * s_im, g_im * s_re - g_re * s_im))
    a2a_start(3, ks_send, ks_recv, block)
    f_re, f_im = spec_f[:, :LANES], spec_f[:, LANES:]
    spread_channels(kf_send, inverse(g_re * f_re + g_im * f_im, g_im * f_re - g_re * f_im))
    for cc in range(PER):
        value = jnp.sum(u_recv[:, cc, :] * sf_recv[pl.ds(cc, n, stride=8), :], axis=(0, 1), keepdims=True)
        kf_send[:, PER + cc, :] = jnp.broadcast_to(value, (n, LANES))
    a2a_start(4, kf_send, kf_recv, block)

    def to_peers(src, dst, send_sem, recv_sem):
        copies = []
        for step in (1, 3, 2):
            copy = pltpu.make_async_remote_copy(
                src_ref=src, dst_ref=dst.at[step - 1], send_sem=send_sem.at[step], recv_sem=recv_sem,
                device_id=(lax.rem(dp + step, 4), me, ch), device_id_type=MESH,
            )
            copy.start()
            copies.append(copy)
        return copies

    a2a_wait(3, ks_recv)
    corr_st = gather_channels(ks_recv)
    f_send[...] = corr_st.astype(BF)
    f_copies = to_peers(f_send, f_recv, f_send_sem, f_recv_sem)

    a2a_wait(4, kf_recv)
    skips = jnp.concatenate([kf_recv[:, PER + cc, :] for cc in range(PER)], axis=0)
    e_send[...] = skips.T[:8]
    e_copies = to_peers(e_send, e_recv, e_send_sem, e_recv_sem)
    gsig_ref[...] = (gather_channels(kf_recv) + skip_t * gradu_t[...]).T.astype(BF)
    outs[1].start()

    pltpu.make_async_copy(g_recv, g_recv, g_sem.at[1]).wait()
    outs[3].start()

    pltpu.make_async_copy(f_recv, f_recv, f_recv_sem).wait()
    sums = corr_st
    for k in range(3):
        sums = sums + f_recv[k].astype(F32)
    gfilt_ref[...] = sums.T
    outs[2].start()

    pltpu.make_async_copy(e_recv, e_recv, e_recv_sem).wait()
    gskip_ref[...] = e_send[...] + e_recv[0] + e_recv[1] + e_recv[2]
    outs[4].start()

    for sub in range(SUB):
        for qq in range(2):
            for hh in range(2):
                @pl.when(to_other(qq))
                def _():
                    cot_copy(sub, qq, hh).wait_send()
    for qq in range(2):
        for hh in range(2):
            @pl.when((2 * ch + qq == dp) & (ch != hh))
            def _():
                own_copy(qq, hh).wait_send()
    a2a_wait_send(0, sf_send, 8)
    for k, src in ((1, c_send), (2, u_send), (3, ks_send), (4, kf_send)):
        a2a_wait_send(k, src, 1)
    w_copy.wait_send()
    pre0_copy.wait_send()
    for copy in pre_copies + ret_copies + f_copies + e_copies:
        copy.wait_send()

    def b_sent(count):
        part = b_send.at[:, pl.ds(0, count * LANES)]
        pltpu.make_async_copy(part, part, b_sem.at[0]).wait()

    @pl.when(me < n_own)
    def _():
        b_sent(n_own - 1)
        for step in (1, 3, 2):
            q_copy(step).wait_send()

        def sent(d, _):
            pltpu.make_async_copy(g_send, g_send, g_sem.at[0]).wait()
            return 0

        lax.fori_loop(1, n, sent, 0)

    @pl.when(me >= n_own)
    def _():
        b_sent(n_own)

    for out in outs:
        out.wait()


def received(copy, ref):
    copy.wait_recv()
    return ref[...].astype(F32)


def finish_kernel(
    gsig_in, ggat_in, gfilt_in, gbank_in, gskip_in,
    gsig_out, ggat_out, gfilt_out, gskip_out, ga_out, gb_out,
    gsig_ref, ggat_ref, gfilt_ref, gbank_ref, gskip_ref, ga_ref, gb_ref, in_sem, out_sem,
):
    max_rank, half = gb_ref.shape[1:]
    width = ga_ref.shape[2]
    g_size = 2 * max_rank
    up_chunks = half // LANES
    a_chunks = -(-width // LANES)
    pairs = (
        (gbank_in, gbank_ref), (gfilt_in, gfilt_ref), (gsig_in, gsig_ref), (ggat_in, ggat_ref),
        (gskip_in.at[pl.ds(0, 1)], gskip_ref),
    )
    loads = [pltpu.make_async_copy(s, d, in_sem.at[i]) for i, (s, d) in enumerate(pairs)]
    for load in loads:
        load.start()
    pairs = (
        (gb_ref, gb_out), (gfilt_ref, gfilt_out), (gsig_ref, gsig_out), (ggat_ref, ggat_out),
        (gskip_ref, gskip_out), (ga_ref, ga_out),
    )
    stores = [pltpu.make_async_copy(s, d, out_sem.at[i]) for i, (s, d) in enumerate(pairs)]
    loads[0].wait()

    def place(p, _):
        block = gbank_ref[pl.ds(pl.multiple_of(p * g_size, g_size), g_size), :].astype(F32)
        where = pl.ds(pl.multiple_of(p * LANES, LANES), LANES)
        gb_ref[0, :, where] = block[:max_rank]
        gb_ref[1, :, where] = block[max_rank:]
        return 0

    lax.fori_loop(0, up_chunks, place, 0, unroll=4)
    stores[0].start()
    for k in range(1, 5):
        loads[k].wait()
        stores[k].start()
    size = min(LANES, width)
    for k in range(a_chunks):
        at = (up_chunks + k) * g_size
        block = gbank_ref[at:at + g_size, :].astype(F32)
        ga_ref[0, :, k * size:(k + 1) * size] = block[:max_rank, :size]
        ga_ref[1, :, k * size:(k + 1) * size] = block[max_rank:, :size]
    stores[5].start()
    for store in stores:
        store.wait()


def local(
    signal, gating, cotangent, filt, skip, output_projection,
    adapter_down_bank, adapter_up_bank, adapter_index, sequence_rank, real_length,
):
    n = lax.axis_size("seq")
    width = signal.shape[2]
    half = cotangent.shape[2]
    cols = output_projection.shape[1] // 2
    max_rank = adapter_up_bank.shape[1]
    a_chunks = -(-width // LANES)
    n_own = half // LANES + a_chunks
    piece = LANES // SUB
    consts = [jnp.asarray(t) for t in tables(n)]
    rows = consts[4].shape[0]
    vmem = pl.BlockSpec(memory_space=pltpu.VMEM)
    smem = pl.BlockSpec(memory_space=pltpu.SMEM)
    hbm = pl.BlockSpec(memory_space=pltpu.HBM)
    dma = pltpu.SemaphoreType.DMA
    arrays = [
        signal[0], gating[0], cotangent[0], filt, skip[None], output_projection,
        jnp.swapaxes(adapter_down_bank, 1, 2), adapter_up_bank, *consts,
    ]
    block = pltpu.VMEM((n, PER, LANES), F32)
    eight = pltpu.VMEM((8 * n, LANES), F32)
    two = pltpu.VMEM((n, 2 * PER, LANES), F32)
    wide = pltpu.VMEM((width, LANES), F32)
    spec = pltpu.VMEM((PER * rows, 2 * LANES), F32)
    rank = pltpu.VMEM((max_rank, LANES), F32)
    outs = pl.pallas_call(
        functools.partial(kernel, n),
        out_shape=(
            jax.ShapeDtypeStruct((LANES, width), BF),
            jax.ShapeDtypeStruct((LANES, width), BF),
            jax.ShapeDtypeStruct((LANES, width), F32),
            jax.ShapeDtypeStruct((2 * max_rank * n_own, LANES), BF),
            jax.ShapeDtypeStruct((8, width), F32),
        ),
        in_specs=[smem] * 3 + [hbm] * len(arrays),
        out_specs=(hbm,) * 5,
        scratch_shapes=[
            pltpu.VMEM((LANES, width), BF),
            pltpu.VMEM((LANES, width), BF),
            pltpu.VMEM((LANES, width), F32),
            pltpu.VMEM((8, width), F32),
        ] + [pltpu.VMEM(a.shape, a.dtype) for a in arrays] + [
            pltpu.VMEM((LANES, half), BF),
            wide, wide, wide, spec, spec, spec,
            eight, eight, block, block, block, block, block, block, two, two,
            pltpu.VMEM((LANES, cols), BF),
            pltpu.VMEM((SUB, 3, piece, cols), BF),
            pltpu.VMEM((width, cols), BF),
            pltpu.VMEM((LANES, width), BF),
            pltpu.VMEM((LANES, width), BF),
            pltpu.VMEM((SUB, 3 * piece, width), BF),
            pltpu.VMEM((SUB, 3 * piece, width), BF),
            pltpu.VMEM((SUB, 3 * piece, width), BF),
            pltpu.VMEM((3, LANES, width), BF),
            rank, rank, rank, rank,
            pltpu.VMEM((max_rank, n_own * LANES), BF),
            pltpu.VMEM((16 * n, LANES), BF),
            pltpu.VMEM((2 * max_rank, LANES), F32),
            pltpu.VMEM((3, 2 * max_rank, LANES), F32),
            pltpu.VMEM((2 * max_rank, LANES), BF),
            pltpu.VMEM((2 * max_rank * n_own, LANES), BF),
            pltpu.VMEM((width, LANES), BF),
            pltpu.VMEM((3, width, LANES), BF),
            pltpu.VMEM((8, width), F32),
            pltpu.VMEM((3, 8, width), F32),
            dma((len(arrays),)), dma((5,)), dma((5,)), dma((5,)), dma((SUB, 4)), dma((SUB,)), dma((2,)), dma((2,)),
            dma((2,)), dma((SUB,)), dma((SUB,)), dma((SUB, 4)), dma, dma((2,)), dma((2,)), dma((2,)),
            dma((4,)), dma, dma((2,)), dma((4,)), dma, dma((4,)), dma,
        ],
        compiler_params=pltpu.CompilerParams(
            collective_id=0, has_side_effects=True, vmem_limit_bytes=VMEM_LIMIT
        ),
    )(adapter_index, sequence_rank, real_length, *arrays)
    grad_signal, grad_gating, grad_filt, grad_skip, grad_a, grad_b = pl.pallas_call(
        finish_kernel,
        out_shape=(
            jax.ShapeDtypeStruct((LANES, width), BF),
            jax.ShapeDtypeStruct((LANES, width), BF),
            jax.ShapeDtypeStruct((LANES, width), F32),
            jax.ShapeDtypeStruct((1, width), F32),
            jax.ShapeDtypeStruct((2, max_rank, width), F32),
            jax.ShapeDtypeStruct((2, max_rank, half), F32),
        ),
        in_specs=[hbm] * 5,
        out_specs=(hbm,) * 6,
        scratch_shapes=[
            pltpu.VMEM((LANES, width), BF), pltpu.VMEM((LANES, width), BF), pltpu.VMEM((LANES, width), F32),
            pltpu.VMEM((2 * max_rank * n_own, LANES), BF), pltpu.VMEM((1, width), F32),
            pltpu.VMEM((2, max_rank, width), F32), pltpu.VMEM((2, max_rank, half), F32),
            dma((5,)), dma((6,)),
        ],
        compiler_params=pltpu.CompilerParams(vmem_limit_bytes=VMEM_LIMIT),
    )(*outs)
    return (grad_signal[None], grad_gating[None], grad_filt, grad_skip[0], jnp.swapaxes(grad_a, 1, 2), grad_b)


def solution(mesh):
    placed = (
        P("dp", "seq", "chan"), P("dp", "seq", "chan"), P("dp", "seq", "chan"), P("seq", "chan"),
        P("chan"), P("chan", "dp"), P(None, "chan", None), P(None, None, "chan"),
        P("dp"), P("dp"), P("dp"),
    )
    return jax.shard_map(
        local,
        mesh=mesh,
        in_specs=placed,
        out_specs=(
            P("dp", "seq", "chan"), P("dp", "seq", "chan"), P("seq", "chan"), P("chan"),
            P(None, "chan", None), P(None, None, "chan"),
        ),
        check_vma=False,
    )
```

time: 113 us -> 87.8 us (0.78)
  local copies, waits for them, and re-layouts: 15 us -> 0 us
  Pallas kernels: 94 us -> 84.5 us
    unnamed x32 -> x0, local copies, waits for them, and re-layouts: 14.4 us -> none
    pallas_call x1, Pallas kernels: 94 us -> 82.4 us  [local(): pl.pallas_call(functools.partial(kernel, n), out_shape=(jax.ShapeDtypeStr...]
    pallas_call x0 -> x1, Pallas kernels: none -> 2.03 us  [local(): pl.pallas_call(finish_kernel, out_shape=(jax.ShapeDtypeStruct((LANES, wid...]
where the time goes in v2:
time: 87.8 us; the launch traced here: 87 us
  Pallas kernels  84.5 us (96%)
  between operations  2.58 us (3%)
    pallas_call x1, Pallas kernels, local(): pl.pallas_call(functools.partial(kernel, n), out_shape=(jax.ShapeDtypeStr...  82.4 us
    pallas_call x1, Pallas kernels, local(): pl.pallas_call(finish_kernel, out_shape=(jax.ShapeDtypeStruct((LANES, wid...  2.03 us

profile of v2, /device:TPU:6, one launch (start us, length us, event | category | flops | bytes accessed | tf_op | source)
XLA Modules:
  0.0 87.0 jit_solution(7633939888495256040)
XLA Ops:
  2.6 82.4 %shard_map.208 = (bf16[128,256]{1,0:T(8,128)(2,1)}, bf16[128,256]{1,0:T(8,128)(2,1)}, f32[128,256]{1,0:T(8,128)}, bf16[1088,128]{1,0:T(8,128)(2,1)}, f32[8,256]{1,0:T(8,128)}) custom-call(s32[1]{0:T(128)S(6)} %copy.23.index_ref, s32[1]{0:T(128)S(6)} %copy.24.rank_ref, s32[1]{0:T(128)S(6)} %copy.25.length_ref, bf16[128,256]{1,0:T(8,128)(2,1)} %bitcast.10, ...), custom_call_target="tpu_custom_call" | custom-call | tf_op jit(solution)/shard_map/pallas_call | solution.py:594
  85.0 2.0 %shard_map.209 = (bf16[128,256]{1,0:T(8,128)(2,1)}, bf16[128,256]{1,0:T(8,128)(2,1)}, f32[128,256]{1,0:T(8,128)}, f32[1,256]{1,0:T(1,128)}, f32[2,16,256]{2,1,0:T(8,128)}, /*index=5*/f32[2,16,4096]{2,1,0:T(8,128)}) custom-call(bf16[128,256]{1,0:T(8,128)(2,1)} %get-tuple-element.17.gsig_in, bf16[128,256]{1,0:T(8,128)(2,1)} %get-tuple-element.18.ggat_in, ...), custom_call_target="tpu_custom_call" | custom-call | tf_op jit(solution)/shard_map/pallas_call | solution.py:642

commit v3 on v2

--- a/solution.py
+++ b/solution.py
@@ -81,12 +81,13 @@
     t1_ref, t2_ref, t2b_ref, t1b_ref, tc_ref, ts_ref,
     masked, sig_t, gate_t, gradu_t, spec_s, spec_f, spec_g,
     sf_send, sf_recv, c_send, c_recv, u_send, u_recv, ks_send, ks_recv, kf_send, kf_recv,
-    m_own, m_recv, w_recv, pre0_send, pre0_recv, pre_send, pre_recv, ret_send, ret_recv,
+    m_own, m_recv, m_far, w_far, far_send, far_recv, w_recv, pre0_send, pre0_recv, pre_send, pre_recv, ret_send, ret_recv,
     d_send, d_recv, r_send, r_recv,
-    b_send, b_recv, q_send, q_recv, g_send, g_recv, f_send, f_recv, e_send, e_recv,
+    b_send, b_recv, q_send, q_recv, g_send, g_recv, f_send, f_recv, corr_st, h_send, h_recv, e_send, e_recv,
     in_sem, out_sem, a2a_send_sem, a2a_recv_sem, m_send_sem, m_recv_sem, own_sem, w_sem, pre0_sem,
     pre_send_sem, pre_recv_sem, ret_send_sem, ret_recv_sem, d_sem, r_sem, b_sem,
     q_send_sem, q_recv_sem, g_sem, f_send_sem, f_recv_sem, e_send_sem, e_recv_sem,
+    h_send_sem, h_recv_sem, far_sem, wf_sem, wy_send_sem, wy_recv_sem, fr_send_sem, fr_recv_sem,
 ):
     dp = lax.axis_index("dp")
     me = lax.axis_index("seq")
@@ -94,6 +95,16 @@
     other = 1 - ch
     plane = n // 2
     zl, spot = lax.div(me, plane), lax.rem(me, plane)
+    group = m_far.shape[0]
+    nx = group // 2
+    ny = plane // nx
+    y, x = lax.div(spot, nx), lax.rem(spot, nx)
+    g = zl * nx + x
+    far_cols = m_far.shape[2]
+
+    def member(k):
+        return lax.div(k, nx) * plane + y * nx + lax.rem(k, nx)
+
     width = w_ref.shape[0]
     cols = w_ref.shape[1] // 2
     half = cot_ref.shape[1]
@@ -120,6 +131,12 @@
         return 0
 
     lax.fori_loop(1, n, greet, 0, unroll=9 if n == 64 else 1)
+    for z in range(2):
+        for k in range(1, nx):
+            pl.semaphore_signal(
+                barrier, inc=1, device_id=(dp, member(z * nx + lax.rem(x + k, nx)), other),
+                device_id_type=MESH,
+            )
 
     pairs = (
         (signal_hbm, signal_ref), (filt_hbm, filt_ref), (cot_hbm, cot_ref), (up_hbm, up_ref),
@@ -144,19 +161,16 @@
     pick1 = index_ref[0].astype(F32)
     pick0 = 1.0 - pick1
 
-    pl.semaphore_wait(barrier, n - 1 + 14)
+    pl.semaphore_wait(barrier, n - 1 + 14 + 2 * (nx - 1))
 
     def cot_copy(sub, qq, hh):
         q = 2 * ch + qq
-        step = lax.rem(q - dp + 4, 4)
-        odd = lax.rem(step, 2)
-        to_z = lax.div(step, 3) + (1 - odd) * (1 - zl)
         return pltpu.make_async_remote_copy(
             src_ref=cot_hbm.at[pl.ds(sub * piece, piece), pl.ds((2 * qq + hh) * cols, cols)],
-            dst_ref=m_recv.at[sub, odd * zl + (1 - odd) * 2],
+            dst_ref=m_recv.at[sub, zl],
             send_sem=m_send_sem.at[sub, 2 * qq + hh],
             recv_sem=m_recv_sem.at[sub],
-            device_id=(q, to_z * plane + spot, hh),
+            device_id=(q, lax.div(lax.rem(q - dp + 4, 4), 3) * plane + spot, hh),
             device_id_type=MESH,
         )
 
@@ -171,7 +185,7 @@
         )
 
     def to_other(qq):
-        return 2 * ch + qq != dp
+        return lax.rem(2 * ch + qq - dp + 4, 2) == 1
 
     for sub in range(SUB):
         for qq in range(2):
@@ -190,6 +204,36 @@
                 pltpu.make_async_copy(
                     cot_hbm.at[:, pl.ds((2 * qq + hh) * cols, cols)], m_own, own_sem.at[1]
                 ).start()
+
+    far = lax.rem(dp + 2, 4)
+    slice_rows = width // ny
+    my_slice = pl.ds(pl.multiple_of(y * slice_rows, slice_rows), slice_rows)
+
+    wf_copy = pltpu.make_async_remote_copy(
+        src_ref=w_hbm.at[my_slice, pl.ds(pl.multiple_of(g * far_cols, far_cols), far_cols)],
+        dst_ref=w_far.at[my_slice, :],
+        send_sem=wf_sem.at[0], recv_sem=wf_sem.at[1], device_id=(far, me, ch), device_id_type=MESH,
+    )
+    wf_copy.start()
+
+    def far_copy(d, c):
+        k = lax.rem(g + d, group)
+        at = lax.rem(far, 2) * 2 * cols + k * far_cols
+        src = cot_hbm.at[:, pl.ds(pl.multiple_of(at, far_cols), far_cols)]
+        if d == 0 and c == 0:
+            return pltpu.make_async_copy(src, m_far.at[d], far_sem.at[1])
+        return pltpu.make_async_remote_copy(
+            src_ref=src, dst_ref=m_far.at[d], send_sem=far_sem.at[0], recv_sem=far_sem.at[1],
+            device_id=(dp, member(k), lax.rem(ch + c, 2)), device_id_type=MESH,
+        )
+
+    holds_far = ch == lax.div(far, 2)
+
+    @pl.when(holds_far)
+    def _():
+        for d in range(group):
+            for c in range(2):
+                far_copy(d, c).start()
 
     def to_chan(src, dst, send_sem, recv_sem):
         return pltpu.make_async_remote_copy(
@@ -233,6 +277,17 @@
 
     a2a_start(0, sf_send, sf_recv, eight)
 
+    wf_copy.wait_recv()
+    wy_copies = []
+    for k in range(1, ny):
+        copy = pltpu.make_async_remote_copy(
+            src_ref=w_far.at[my_slice, :], dst_ref=w_far.at[my_slice, :],
+            send_sem=wy_send_sem.at[k], recv_sem=wy_recv_sem,
+            device_id=(dp, zl * plane + lax.rem(y + k, ny) * nx + x, ch), device_id_type=MESH,
+        )
+        copy.start()
+        wy_copies.append(copy)
+
     for load in loads[2:]:
         load.wait()
     masked[...] = (cot_ref[...].astype(F32) * live_col).astype(BF)
@@ -258,7 +313,7 @@
 
     def project(sub):
         pltpu.make_async_copy(m_recv.at[sub], m_recv.at[sub], m_recv_sem.at[sub]).wait()
-        part = m_recv[sub].reshape(3 * piece, cols)
+        part = m_recv[sub].reshape(2 * piece, cols)
         pre_send[sub] = dot_t(part, w_recv[...]).astype(BF)
         copy = to_chan(pre_send.at[sub], pre_recv.at[sub], pre_send_sem.at[sub], pre_recv_sem.at[sub])
         copy.start()
@@ -268,13 +323,12 @@
     def give_back(sub, mine):
         pre_copies[sub].wait_recv()
         ret_send[sub] = (mine + pre_recv[sub].astype(F32)).astype(BF)
-        near, far = lax.rem(dp + 3 - 2 * zl, 4), lax.rem(dp + 2, 4)
-        for slot, (b, z, back) in enumerate(((near, 0, zl), (near, 1, zl), (far, 1 - zl, 2))):
+        for slot in range(2):
             copy = pltpu.make_async_remote_copy(
                 src_ref=ret_send.at[sub, pl.ds(slot * piece, piece)],
-                dst_ref=ret_recv.at[back, pl.ds(sub * piece, piece)],
+                dst_ref=ret_recv.at[zl, pl.ds(sub * piece, piece)],
                 send_sem=ret_send_sem.at[sub, slot], recv_sem=ret_recv_sem,
-                device_id=(b, z * plane + spot, ch), device_id_type=MESH,
+                device_id=(lax.rem(dp + 3 - 2 * zl, 4), slot * plane + spot, ch), device_id_type=MESH,
             )
             copy.start()
             ret_copies.append(copy)
@@ -318,6 +372,30 @@
     d_copy.wait()
     back_rank = (2.0 * (d_send[...] + d_recv[...]) * keep).astype(BF)
 
+    pltpu.make_async_copy(m_far, m_far, far_sem.at[1]).wait()
+    if ny > 1:
+        rest = w_far.at[pl.ds(0, (ny - 1) * slice_rows), :]
+        pltpu.make_async_copy(rest, rest, wy_recv_sem).wait()
+    far_part = dot_t(m_far[...].reshape(group * LANES, far_cols), w_far[...])
+    far_send[...] = far_part[LANES:].astype(BF)
+    own_part = own_part + far_part[:LANES]
+    far_copies = []
+    for d in range(1, group):
+        copy = pltpu.make_async_remote_copy(
+            src_ref=far_send.at[pl.ds((d - 1) * LANES, LANES), :], dst_ref=far_recv.at[d - 1],
+            send_sem=fr_send_sem.at[d], recv_sem=fr_recv_sem,
+            device_id=(dp, member(lax.rem(g + group - d, group)), ch), device_id_type=MESH,
+        )
+        copy.start()
+        far_copies.append(copy)
+
+    mine = project(0)
+    for sub in range(1, SUB):
+        after = project(sub)
+        give_back(sub - 1, mine)
+        mine = after
+    give_back(SUB - 1, mine)
+
     a2a_wait(1, c_recv)
     inner_t = gather_channels(c_recv) + skip_t * sig_t[...]
     gated_t = (gate_t[...] * inner_t).astype(BF)
@@ -326,6 +404,19 @@
     r_copy.start()
     b_send[:, half:half + width] = dot_t(back_rank, gated_t).astype(BF)
 
+    grad_y = own_part + received(pre0_copy, pre0_recv)
+    pltpu.make_async_copy(ret_recv, ret_recv, ret_recv_sem).wait()
+    pltpu.make_async_copy(far_recv, far_recv, fr_recv_sem).wait()
+    for k in range(2):
+        grad_y = grad_y + ret_recv[k].astype(F32)
+    for k in range(group - 1):
+        grad_y = grad_y + far_recv[k].astype(F32)
+    grad_y = grad_y.T * live_row + dot_0(down_sel, back_rank)
+    grad_u = grad_y * gate_t[...]
+    gradu_t[...] = grad_u
+    for cc in range(PER):
+        u_send[:, cc, :] = gradu_t[cc * n:(cc + 1) * n, :]
+    a2a_start(2, u_send, u_recv, block)
     r_copy.wait()
     fwd_rank = (2.0 * (r_send[...] + r_recv[...]) * keep).astype(BF)
     b_send[:, :half] = dot(fwd_rank, masked[...]).astype(BF)
@@ -355,12 +446,15 @@
 
     lax.fori_loop(0, n_own, share, 0)
 
-    mine = project(0)
-    for sub in range(1, SUB):
-        after = project(sub)
-        give_back(sub - 1, mine)
-        mine = after
-    give_back(SUB - 1, mine)
+    ggat_ref[...] = (grad_y * inner_t).T.astype(BF)
+    outs = [
+        pltpu.make_async_copy(s, d, out_sem.at[i])
+        for i, (s, d) in enumerate((
+            (ggat_ref, ggat_hbm), (gsig_ref, gsig_hbm), (gfilt_ref, gfilt_hbm), (g_recv, gbank_hbm),
+            (gskip_ref, gskip_hbm),
+        ))
+    ]
+    outs[0].start()
 
     is_owner = me < n_own
 
@@ -379,44 +473,6 @@
         q_send[...] = jnp.concatenate([acc * pick0, acc * pick1], axis=0)
         for step in (1, 3, 2):
             q_copy(step).start()
-
-    grad_y = own_part + received(pre0_copy, pre0_recv)
-    pltpu.make_async_copy(ret_recv, ret_recv, ret_recv_sem).wait()
-    for k in range(3):
-        grad_y = grad_y + ret_recv[k].astype(F32)
-    grad_y = grad_y.T * live_row + dot_0(down_sel, back_rank)
-    grad_u = grad_y * gate_t[...]
-    gradu_t[...] = grad_u
-    for cc in range(PER):
-        u_send[:, cc, :] = gradu_t[cc * n:(cc + 1) * n, :]
-    a2a_start(2, u_send, u_recv, block)
-    ggat_ref[...] = (grad_y * inner_t).T.astype(BF)
-    outs = [
-        pltpu.make_async_copy(s, d, out_sem.at[i])
-        for i, (s, d) in enumerate((
-            (ggat_ref, ggat_hbm), (gsig_ref, gsig_hbm), (gfilt_ref, gfilt_hbm), (g_recv, gbank_hbm),
-            (gskip_ref, gskip_hbm),
-        ))
-    ]
-    outs[0].start()
-
-    g_size = 2 * max_rank
-
-    @pl.when(is_owner)
-    def _():
-        pltpu.make_async_copy(q_recv, q_recv, q_recv_sem).wait()
-        g_send[...] = (q_send[...] + q_recv[0] + q_recv[1] + q_recv[2]).astype(BF)
-        at = pl.ds(pl.multiple_of(me * g_size, g_size), g_size)
-
-        def spread(d, _):
-            pltpu.make_async_remote_copy(
-                src_ref=g_send, dst_ref=g_recv.at[at, :], send_sem=g_sem.at[0], recv_sem=g_sem.at[1],
-                device_id=(dp, lax.rem(me + d, n), ch), device_id_type=MESH,
-            ).start()
-            return 0
-
-        lax.fori_loop(1, n, spread, 0, unroll=9 if n == 64 else 1)
-        pltpu.make_async_copy(g_send, g_recv.at[at, :], g_sem.at[1]).start()
 
     a2a_wait(2, u_recv)
     forward(lambda cc: u_recv[:, cc, :], spec_g)
@@ -431,6 +487,24 @@
         kf_send[:, PER + cc, :] = jnp.broadcast_to(value, (n, LANES))
     a2a_start(4, kf_send, kf_recv, block)
 
+    g_size = 2 * max_rank
+
+    @pl.when(is_owner)
+    def _():
+        pltpu.make_async_copy(q_recv, q_recv, q_recv_sem).wait()
+        g_send[...] = (q_send[...] + q_recv[0] + q_recv[1] + q_recv[2]).astype(BF)
+        at = pl.ds(pl.multiple_of(me * g_size, g_size), g_size)
+
+        def spread(d, _):
+            pltpu.make_async_remote_copy(
+                src_ref=g_send, dst_ref=g_recv.at[at, :], send_sem=g_sem.at[0], recv_sem=g_sem.at[1],
+                device_id=(dp, lax.rem(me + d, n), ch), device_id_type=MESH,
+            ).start()
+            return 0
+
+        lax.fori_loop(1, n, spread, 0, unroll=9 if n == 64 else 1)
+        pltpu.make_async_copy(g_send, g_recv.at[at, :], g_sem.at[1]).start()
+
     def to_peers(src, dst, send_sem, recv_sem):
         copies = []
         for step in (1, 3, 2):
@@ -443,25 +517,48 @@
         return copies
 
     a2a_wait(3, ks_recv)
-    corr_st = gather_channels(ks_recv)
-    f_send[...] = corr_st.astype(BF)
-    f_copies = to_peers(f_send, f_recv, f_send_sem, f_recv_sem)
+    quarter = width // 4
+    corr_st[...] = gather_channels(ks_recv)
+    f_send[...] = corr_st[...].astype(BF)
+    f_copies = []
+    for step in (1, 3, 2):
+        q = lax.rem(dp + step, 4)
+        copy = pltpu.make_async_remote_copy(
+            src_ref=f_send.at[pl.ds(pl.multiple_of(q * quarter, quarter), quarter), :],
+            dst_ref=f_recv.at[step - 1], send_sem=f_send_sem.at[step], recv_sem=f_recv_sem,
+            device_id=(q, me, ch), device_id_type=MESH,
+        )
+        copy.start()
+        f_copies.append(copy)
 
     a2a_wait(4, kf_recv)
     skips = jnp.concatenate([kf_recv[:, PER + cc, :] for cc in range(PER)], axis=0)
     e_send[...] = skips.T[:8]
     e_copies = to_peers(e_send, e_recv, e_send_sem, e_recv_sem)
+
+    pltpu.make_async_copy(f_recv, f_recv, f_recv_sem).wait()
+    my_quarter = pl.ds(pl.multiple_of(dp * quarter, quarter), quarter)
+    sums = corr_st[my_quarter, :]
+    for k in range(3):
+        sums = sums + f_recv[k].astype(F32)
+    h_send[...] = sums.astype(BF)
+    h_copies = []
+    for step in (1, 3, 2):
+        copy = pltpu.make_async_remote_copy(
+            src_ref=h_send, dst_ref=h_recv.at[my_quarter, :], send_sem=h_send_sem.at[step],
+            recv_sem=h_recv_sem, device_id=(lax.rem(dp + step, 4), me, ch), device_id_type=MESH,
+        )
+        copy.start()
+        h_copies.append(copy)
+    pltpu.make_async_copy(h_send, h_recv.at[my_quarter, :], h_recv_sem).start()
     gsig_ref[...] = (gather_channels(kf_recv) + skip_t * gradu_t[...]).T.astype(BF)
     outs[1].start()
 
     pltpu.make_async_copy(g_recv, g_recv, g_sem.at[1]).wait()
     outs[3].start()
 
-    pltpu.make_async_copy(f_recv, f_recv, f_recv_sem).wait()
-    sums = corr_st
-    for k in range(3):
-        sums = sums + f_recv[k].astype(F32)
-    gfilt_ref[...] = sums.T
+    pltpu.make_async_copy(h_recv, h_recv, h_recv_sem).wait()
+    gfilt_ref[...] = h_recv[...].astype(F32).T
     outs[2].start()
 
     pltpu.make_async_copy(e_recv, e_recv, e_recv_sem).wait()
@@ -484,8 +581,17 @@
         a2a_wait_send(k, src, 1)
     w_copy.wait_send()
     pre0_copy.wait_send()
-    for copy in pre_copies + ret_copies + f_copies + e_copies:
+    wf_copy.wait_send()
+    for copy in wy_copies + far_copies + pre_copies + ret_copies + f_copies + h_copies + e_copies:
         copy.wait_send()
+
+    @pl.when(holds_far)
+    def _():
+        def sent(d, _):
+            pltpu.make_async_copy(m_far.at[0], m_far.at[0], far_sem.at[0]).wait()
+            return 0
+
+        lax.fori_loop(1, 2 * group, sent, 0)
 
     def b_sent(count):
         part = b_send.at[:, pl.ds(0, count * LANES)]
@@ -575,6 +681,8 @@
     a_chunks = -(-width // LANES)
     n_own = half // LANES + a_chunks
     piece = LANES // SUB
+    group = 2 * min(4, n // 2)
+    far_cols = 2 * cols // group
     consts = [jnp.asarray(t) for t in tables(n)]
     rows = consts[4].shape[0]
     vmem = pl.BlockSpec(memory_space=pltpu.VMEM)
@@ -612,14 +720,18 @@
             wide, wide, wide, spec, spec, spec,
             eight, eight, block, block, block, block, block, block, two, two,
             pltpu.VMEM((LANES, cols), BF),
-            pltpu.VMEM((SUB, 3, piece, cols), BF),
+            pltpu.VMEM((SUB, 2, piece, cols), BF),
+            pltpu.VMEM((group, LANES, far_cols), BF),
+            pltpu.VMEM((width, far_cols), BF),
+            pltpu.VMEM(((group - 1) * LANES, width), BF),
+            pltpu.VMEM((group - 1, LANES, width), BF),
             pltpu.VMEM((width, cols), BF),
             pltpu.VMEM((LANES, width), BF),
             pltpu.VMEM((LANES, width), BF),
-            pltpu.VMEM((SUB, 3 * piece, width), BF),
-            pltpu.VMEM((SUB, 3 * piece, width), BF),
-            pltpu.VMEM((SUB, 3 * piece, width), BF),
-            pltpu.VMEM((3, LANES, width), BF),
+            pltpu.VMEM((SUB, 2 * piece, width), BF),
+            pltpu.VMEM((SUB, 2 * piece, width), BF),
+            pltpu.VMEM((SUB, 2 * piece, width), BF),
+            pltpu.VMEM((2, LANES, width), BF),
             rank, rank, rank, rank,
             pltpu.VMEM((max_rank, n_own * LANES), BF),
             pltpu.VMEM((16 * n, LANES), BF),
@@ -628,12 +740,16 @@
             pltpu.VMEM((2 * max_rank, LANES), BF),
             pltpu.VMEM((2 * max_rank * n_own, LANES), BF),
             pltpu.VMEM((width, LANES), BF),
-            pltpu.VMEM((3, width, LANES), BF),
+            pltpu.VMEM((3, width // 4, LANES), BF),
+            wide,
+            pltpu.VMEM((width // 4, LANES), BF),
+            pltpu.VMEM((width, LANES), BF),
             pltpu.VMEM((8, width), F32),
             pltpu.VMEM((3, 8, width), F32),
             dma((len(arrays),)), dma((5,)), dma((5,)), dma((5,)), dma((SUB, 4)), dma((SUB,)), dma((2,)), dma((2,)),
             dma((2,)), dma((SUB,)), dma((SUB,)), dma((SUB, 4)), dma, dma((2,)), dma((2,)), dma((2,)),
             dma((4,)), dma, dma((2,)), dma((4,)), dma, dma((4,)), dma,
+            dma((4,)), dma, dma((2,)), dma((2,)), dma((8,)), dma, dma((group,)), dma,
         ],
         compiler_params=pltpu.CompilerParams(
             collective_id=0, has_side_effects=True, vmem_limit_bytes=VMEM_LIMIT

time: 87.8 us -> 88.4 us (level)
  Pallas kernels: 84.5 us -> 85.6 us
    pallas_call x1, Pallas kernels: 82.4 us -> 83.5 us  [local(): pl.pallas_call(functools.partial(kernel, n), out_shape=(jax.ShapeDtypeStr...]
where the time goes in v3:
time: 88.4 us; the launch traced here: 88.1 us
  Pallas kernels  85.6 us (97%)
  between operations  2.58 us (3%)
    pallas_call x1, Pallas kernels, local(): pl.pallas_call(functools.partial(kernel, n), out_shape=(jax.ShapeDtypeStr...  83.5 us
    pallas_call x1, Pallas kernels, local(): pl.pallas_call(finish_kernel, out_shape=(jax.ShapeDtypeStruct((LANES, wid...  2.03 us

profile of v3, /device:TPU:6, one launch (start us, length us, event | category | flops | bytes accessed | tf_op | source)
XLA Modules:
  0.0 88.1 jit_solution(18037493529229824164)
XLA Ops:
  2.6 83.5 %shard_map.208 = (bf16[128,256]{1,0:T(8,128)(2,1)}, bf16[128,256]{1,0:T(8,128)(2,1)}, f32[128,256]{1,0:T(8,128)}, bf16[1088,128]{1,0:T(8,128)(2,1)}, f32[8,256]{1,0:T(8,128)}) custom-call(s32[1]{0:T(128)S(6)} %copy.23.index_ref, s32[1]{0:T(128)S(6)} %copy.24.rank_ref, s32[1]{0:T(128)S(6)} %copy.25.length_ref, bf16[128,256]{1,0:T(8,128)(2,1)} %bitcast.10, ...), custom_call_target="tpu_custom_call" | custom-call | tf_op jit(solution)/shard_map/pallas_call | solution.py:702
  86.1 2.0 %shard_map.209 = (bf16[128,256]{1,0:T(8,128)(2,1)}, bf16[128,256]{1,0:T(8,128)(2,1)}, f32[128,256]{1,0:T(8,128)}, f32[1,256]{1,0:T(1,128)}, f32[2,16,256]{2,1,0:T(8,128)}, /*index=5*/f32[2,16,4096]{2,1,0:T(8,128)}) custom-call(bf16[128,256]{1,0:T(8,128)(2,1)} %get-tuple-element.17.gsig_in, bf16[128,256]{1,0:T(8,128)(2,1)} %get-tuple-element.18.ggat_in, ...), custom_call_target="tpu_custom_call" | custom-call | tf_op jit(solution)/shard_map/pallas_call | solution.py:758

commit v4 on v3

--- a/solution.py
+++ b/solution.py
@@ -75,18 +75,18 @@
     index_ref, rank_ref, length_ref,
     signal_hbm, gating_hbm, cot_hbm, filt_hbm, skip_hbm, w_hbm, down_hbm, up_hbm,
     t1_hbm, t2_hbm, t2b_hbm, t1b_hbm, tc_hbm, ts_hbm,
-    gsig_hbm, ggat_hbm, gfilt_hbm, gbank_hbm, gskip_hbm,
-    gsig_ref, ggat_ref, gfilt_ref, gskip_ref,
+    gsig_hbm, ggat_hbm, gfilt_hbm, gbank_hbm,
+    gsig_ref, ggat_ref, gfilt_ref,
     signal_ref, gating_ref, cot_ref, filt_ref, skip_ref, w_ref, down_ref, up_ref,
     t1_ref, t2_ref, t2b_ref, t1b_ref, tc_ref, ts_ref,
     masked, sig_t, gate_t, gradu_t, spec_s, spec_f, spec_g,
     sf_send, sf_recv, c_send, c_recv, u_send, u_recv, ks_send, ks_recv, kf_send, kf_recv,
     m_own, m_recv, m_far, w_far, far_send, far_recv, w_recv, pre0_send, pre0_recv, pre_send, pre_recv, ret_send, ret_recv,
     d_send, d_recv, r_send, r_recv,
-    b_send, b_recv, q_send, q_recv, g_send, g_recv, f_send, f_recv, corr_st, h_send, h_recv, e_send, e_recv,
+    b_send, b_recv, q_send, q_recv, g_send, g_recv, f_send, f_recv, corr_st, h_send, h_recv,
     in_sem, out_sem, a2a_send_sem, a2a_recv_sem, m_send_sem, m_recv_sem, own_sem, w_sem, pre0_sem,
     pre_send_sem, pre_recv_sem, ret_send_sem, ret_recv_sem, d_sem, r_sem, b_sem,
-    q_send_sem, q_recv_sem, g_sem, f_send_sem, f_recv_sem, e_send_sem, e_recv_sem,
+    q_send_sem, q_recv_sem, g_sem, f_send_sem, f_recv_sem,
     h_send_sem, h_recv_sem, far_sem, wf_sem, wy_send_sem, wy_recv_sem, fr_send_sem, fr_recv_sem,
 ):
     dp = lax.axis_index("dp")
@@ -110,6 +110,7 @@
     half = cot_ref.shape[1]
     piece = LANES // SUB
     n_own = b_send.shape[1] // LANES
+    extras = n_own - n // 2
     rows = t1_ref.shape[0] // 2
     a_chunks = -(-width // LANES)
 
@@ -163,89 +164,6 @@
 
     pl.semaphore_wait(barrier, n - 1 + 14 + 2 * (nx - 1))
 
-    def cot_copy(sub, qq, hh):
-        q = 2 * ch + qq
-        return pltpu.make_async_remote_copy(
-            src_ref=cot_hbm.at[pl.ds(sub * piece, piece), pl.ds((2 * qq + hh) * cols, cols)],
-            dst_ref=m_recv.at[sub, zl],
-            send_sem=m_send_sem.at[sub, 2 * qq + hh],
-            recv_sem=m_recv_sem.at[sub],
-            device_id=(q, lax.div(lax.rem(q - dp + 4, 4), 3) * plane + spot, hh),
-            device_id_type=MESH,
-        )
-
-    def own_copy(qq, hh):
-        return pltpu.make_async_remote_copy(
-            src_ref=cot_hbm.at[:, pl.ds((2 * qq + hh) * cols, cols)],
-            dst_ref=m_own,
-            send_sem=own_sem.at[0],
-            recv_sem=own_sem.at[1],
-            device_id=(dp, me, hh),
-            device_id_type=MESH,
-        )
-
-    def to_other(qq):
-        return lax.rem(2 * ch + qq - dp + 4, 2) == 1
-
-    for sub in range(SUB):
-        for qq in range(2):
-            for hh in range(2):
-                @pl.when(to_other(qq))
-                def _():
-                    cot_copy(sub, qq, hh).start()
-    for qq in range(2):
-        for hh in range(2):
-            @pl.when((2 * ch + qq == dp) & (ch != hh))
-            def _():
-                own_copy(qq, hh).start()
-
-            @pl.when((2 * ch + qq == dp) & (ch == hh))
-            def _():
-                pltpu.make_async_copy(
-                    cot_hbm.at[:, pl.ds((2 * qq + hh) * cols, cols)], m_own, own_sem.at[1]
-                ).start()
-
-    far = lax.rem(dp + 2, 4)
-    slice_rows = width // ny
-    my_slice = pl.ds(pl.multiple_of(y * slice_rows, slice_rows), slice_rows)
-
-    wf_copy = pltpu.make_async_remote_copy(
-        src_ref=w_hbm.at[my_slice, pl.ds(pl.multiple_of(g * far_cols, far_cols), far_cols)],
-        dst_ref=w_far.at[my_slice, :],
-        send_sem=wf_sem.at[0], recv_sem=wf_sem.at[1], device_id=(far, me, ch), device_id_type=MESH,
-    )
-    wf_copy.start()
-
-    def far_copy(d, c):
-        k = lax.rem(g + d, group)
-        at = lax.rem(far, 2) * 2 * cols + k * far_cols
-        src = cot_hbm.at[:, pl.ds(pl.multiple_of(at, far_cols), far_cols)]
-        if d == 0 and c == 0:
-            return pltpu.make_async_copy(src, m_far.at[d], far_sem.at[1])
-        return pltpu.make_async_remote_copy(
-            src_ref=src, dst_ref=m_far.at[d], send_sem=far_sem.at[0], recv_sem=far_sem.at[1],
-            device_id=(dp, member(k), lax.rem(ch + c, 2)), device_id_type=MESH,
-        )
-
-    holds_far = ch == lax.div(far, 2)
-
-    @pl.when(holds_far)
-    def _():
-        for d in range(group):
-            for c in range(2):
-                far_copy(d, c).start()
-
-    def to_chan(src, dst, send_sem, recv_sem):
-        return pltpu.make_async_remote_copy(
-            src_ref=src, dst_ref=dst, send_sem=send_sem, recv_sem=recv_sem,
-            device_id=(dp, me, other), device_id_type=MESH,
-        )
-
-    w_copy = to_chan(
-        w_hbm.at[:, pl.ds(pl.multiple_of(other * cols, LANES), cols)], w_recv, w_sem.at[0], w_sem.at[1]
-    )
-    w_copy.start()
-
     def a2a_start(k, src, dst, at):
         def body(d, _):
             j = lax.rem(me + d, n)
@@ -276,6 +194,89 @@
         return j
 
     a2a_start(0, sf_send, sf_recv, eight)
+
+    def cot_copy(sub, qq, hh):
+        q = 2 * ch + qq
+        return pltpu.make_async_remote_copy(
+            src_ref=cot_hbm.at[pl.ds(sub * piece, piece), pl.ds((2 * qq + hh) * cols, cols)],
+            dst_ref=m_recv.at[sub, zl],
+            send_sem=m_send_sem.at[sub, 2 * qq + hh],
+            recv_sem=m_recv_sem.at[sub],
+            device_id=(q, lax.div(lax.rem(q - dp + 4, 4), 3) * plane + spot, hh),
+            device_id_type=MESH,
+        )
+
+    def own_copy(qq, hh):
+        return pltpu.make_async_remote_copy(
+            src_ref=cot_hbm.at[:, pl.ds((2 * qq + hh) * cols, cols)],
+            dst_ref=m_own,
+            send_sem=own_sem.at[0],
+            recv_sem=own_sem.at[1],
+            device_id=(dp, me, hh),
+            device_id_type=MESH,
+        )
+
+    def to_other(qq):
+        return lax.rem(2 * ch + qq - dp + 4, 2) == 1
+
+    for sub in range(SUB):
+        for qq in range(2):
+            for hh in range(2):
+                @pl.when(to_other(qq))
+                def _():
+                    cot_copy(sub, qq, hh).start()
+    for qq in range(2):
+        for hh in range(2):
+            @pl.when((2 * ch + qq == dp) & (ch != hh))
+            def _():
+                own_copy(qq, hh).start()
+
+            @pl.when((2 * ch + qq == dp) & (ch == hh))
+            def _():
+                pltpu.make_async_copy(
+                    cot_hbm.at[:, pl.ds((2 * qq + hh) * cols, cols)], m_own, own_sem.at[1]
+                ).start()
+
+    far = lax.rem(dp + 2, 4)
+    slice_rows = width // ny
+    my_slice = pl.ds(pl.multiple_of(y * slice_rows, slice_rows), slice_rows)
+
+    wf_copy = pltpu.make_async_remote_copy(
+        src_ref=w_hbm.at[my_slice, pl.ds(pl.multiple_of(g * far_cols, far_cols), far_cols)],
+        dst_ref=w_far.at[my_slice, :],
+        send_sem=wf_sem.at[0], recv_sem=wf_sem.at[1], device_id=(far, me, ch), device_id_type=MESH,
+    )
+    wf_copy.start()
+
+    def far_copy(d, c):
+        k = lax.rem(g + d, group)
+        at = lax.rem(far, 2) * 2 * cols + k * far_cols
+        src = cot_hbm.at[:, pl.ds(pl.multiple_of(at, far_cols), far_cols)]
+        if d == 0 and c == 0:
+            return pltpu.make_async_copy(src, m_far.at[d], far_sem.at[1])
+        return pltpu.make_async_remote_copy(
+            src_ref=src, dst_ref=m_far.at[d], send_sem=far_sem.at[0], recv_sem=far_sem.at[1],
+            device_id=(dp, member(k), lax.rem(ch + c, 2)), device_id_type=MESH,
+        )
+
+    holds_far = ch == lax.div(far, 2)
+
+    @pl.when(holds_far)
+    def _():
+        for d in range(group):
+            for c in range(2):
+                far_copy(d, c).start()
+
+    def to_chan(src, dst, send_sem, recv_sem):
+        return pltpu.make_async_remote_copy(
+            src_ref=src, dst_ref=dst, send_sem=send_sem, recv_sem=recv_sem,
+            device_id=(dp, me, other), device_id_type=MESH,
+        )
+
+    w_copy = to_chan(
+        w_hbm.at[:, pl.ds(pl.multiple_of(other * cols, LANES), cols)], w_recv, w_sem.at[0], w_sem.at[1]
+    )
+    w_copy.start()
 
     wf_copy.wait_recv()
     wy_copies = []
@@ -421,42 +422,58 @@
     fwd_rank = (2.0 * (r_send[...] + r_recv[...]) * keep).astype(BF)
     b_send[:, :half] = dot(fwd_rank, masked[...]).astype(BF)
 
-    def share_copy(p):
-        return pltpu.make_async_remote_copy(
-            src_ref=b_send.at[:, pl.ds(pl.multiple_of(p * LANES, LANES), LANES)],
-            dst_ref=b_recv.at[pl.ds(pl.multiple_of(me * 16, 16), 16), :],
-            send_sem=b_sem.at[0], recv_sem=b_sem.at[1], device_id=(dp, p, ch), device_id_type=MESH,
-        )
-
-    def share(d, _):
-        p = lax.rem(me + d, n_own)
-
-        @pl.when(p != me)
+    product = grad_u * sig_t[...]
+    high = product.astype(BF)
+    low = (product - high.astype(F32)).astype(BF)
+    ones = jnp.ones((max_rank, LANES), BF)
+    at = half + a_chunks * LANES
+    b_send[:, at:at + width] = (dot_t(ones, high) + dot_t(ones, low)).astype(BF)
+
+    def share(p, owner):
+        src = b_send.at[:, pl.ds(pl.multiple_of(p * LANES, LANES), LANES)]
+        dst = b_recv.at[pl.ds(pl.multiple_of(me * 16, 16), 16), :]
+
+        @pl.when(owner != me)
         def _():
-            share_copy(p).start()
-
-        @pl.when(p == me)
+            pltpu.make_async_remote_copy(
+                src_ref=src, dst_ref=dst, send_sem=b_sem.at[0], recv_sem=b_sem.at[1],
+                device_id=(dp, owner, ch), device_id_type=MESH,
+            ).start()
+
+        @pl.when(owner == me)
         def _():
-            pltpu.make_async_copy(
-                b_send.at[:, pl.ds(pl.multiple_of(p * LANES, LANES), LANES)],
-                b_recv.at[pl.ds(pl.multiple_of(me * 16, 16), 16), :],
-                b_sem.at[1],
-            ).start()
+            pltpu.make_async_copy(src, dst, b_sem.at[1]).start()
+
+    def share_main(d, _):
+        p = lax.rem(me + d, plane)
+        share(p, p)
         return 0
 
-    lax.fori_loop(0, n_own, share, 0)
+    for k in range(extras):
+        share(plane + k, plane + (k % ny) * nx + k // ny)
+    lax.fori_loop(0, plane, share_main, 0, unroll=4 if n == 64 else 1)
 
     ggat_ref[...] = (grad_y * inner_t).T.astype(BF)
     outs = [
         pltpu.make_async_copy(s, d, out_sem.at[i])
         for i, (s, d) in enumerate((
             (ggat_ref, ggat_hbm), (gsig_ref, gsig_hbm), (gfilt_ref, gfilt_hbm), (g_recv, gbank_hbm),
-            (gskip_ref, gskip_hbm),
         ))
     ]
     outs[0].start()
 
-    is_owner = me < n_own
+    a2a_wait(2, u_recv)
+    forward(lambda cc: u_recv[:, cc, :], spec_g)
+    g_re, g_im = spec_g[:, :LANES], spec_g[:, LANES:]
+    s_re, s_im = spec_s[:, :LANES], spec_s[:, LANES:]
+    spread_channels(ks_send, inverse(g_re * s_re + g_im * s_im, g_im * s_re - g_re * s_im))
+    a2a_start(3, ks_send, ks_recv, block)
+    f_re, f_im = spec_f[:, :LANES], spec_f[:, LANES:]
+    spread_channels(kf_send, inverse(g_re * f_re + g_im * f_im, g_im * f_re - g_re * f_im))
+    a2a_start(4, kf_send, kf_recv, block)
+
+    column = zl * plane + x * ny
+    is_owner = column + y < n_own
 
     def q_copy(step):
         return pltpu.make_async_remote_copy(
@@ -473,48 +490,6 @@
         q_send[...] = jnp.concatenate([acc * pick0, acc * pick1], axis=0)
         for step in (1, 3, 2):
             q_copy(step).start()
-
-    a2a_wait(2, u_recv)
-    forward(lambda cc: u_recv[:, cc, :], spec_g)
-    g_re, g_im = spec_g[:, :LANES], spec_g[:, LANES:]
-    s_re, s_im = spec_s[:, :LANES], spec_s[:, LANES:]
-    spread_channels(ks_send, inverse(g_re * s_re + g_im * s_im, g_im * s_re - g_re * s_im))
-    a2a_start(3, ks_send, ks_recv, block)
-    f_re, f_im = spec_f[:, :LANES], spec_f[:, LANES:]
-    spread_channels(kf_send, inverse(g_re * f_re + g_im * f_im, g_im * f_re - g_re * f_im))
-    for cc in range(PER):
-        value = jnp.sum(u_recv[:, cc, :] * sf_recv[pl.ds(cc, n, stride=8), :], axis=(0, 1), keepdims=True)
-        kf_send[:, PER + cc, :] = jnp.broadcast_to(value, (n, LANES))
-    a2a_start(4, kf_send, kf_recv, block)
-
-    g_size = 2 * max_rank
-
-    @pl.when(is_owner)
-    def _():
-        pltpu.make_async_copy(q_recv, q_recv, q_recv_sem).wait()
-        g_send[...] = (q_send[...] + q_recv[0] + q_recv[1] + q_recv[2]).astype(BF)
-        at = pl.ds(pl.multiple_of(me * g_size, g_size), g_size)
-
-        def spread(d, _):
-            pltpu.make_async_remote_copy(
-                src_ref=g_send, dst_ref=g_recv.at[at, :], send_sem=g_sem.at[0], recv_sem=g_sem.at[1],
-                device_id=(dp, lax.rem(me + d, n), ch), device_id_type=MESH,
-            ).start()
-            return 0
-
-        lax.fori_loop(1, n, spread, 0, unroll=9 if n == 64 else 1)
-        pltpu.make_async_copy(g_send, g_recv.at[at, :], g_sem.at[1]).start()
-
-    def to_peers(src, dst, send_sem, recv_sem):
-        copies = []
-        for step in (1, 3, 2):
-            copy = pltpu.make_async_remote_copy(
-                src_ref=src, dst_ref=dst.at[step - 1], send_sem=send_sem.at[step], recv_sem=recv_sem,
-                device_id=(lax.rem(dp + step, 4), me, ch), device_id_type=MESH,
-            )
-            copy.start()
-            copies.append(copy)
-        return copies
 
     a2a_wait(3, ks_recv)
     quarter = width // 4
@@ -531,10 +506,23 @@
         copy.start()
         f_copies.append(copy)
 
+    g_size = 2 * max_rank
+    bank_rows = pl.ds(pl.multiple_of((column + y) * g_size, g_size), g_size)
+
+    @pl.when(is_owner)
+    def _():
+        pltpu.make_async_copy(q_recv, q_recv, q_recv_sem).wait()
+        g_send[...] = (q_send[...] + q_recv[0] + q_recv[1] + q_recv[2]).astype(BF)
+        for k in range(1, ny):
+            pltpu.make_async_remote_copy(
+                src_ref=g_send, dst_ref=g_recv.at[bank_rows, :], send_sem=g_sem.at[0], recv_sem=g_sem.at[1],
+                device_id=(dp, zl * plane + lax.rem(y + k, ny) * nx + x, ch), device_id_type=MESH,
+            ).start()
+        pltpu.make_async_copy(g_send, g_recv.at[bank_rows, :], g_sem.at[1]).start()
+
     a2a_wait(4, kf_recv)
-    skips = jnp.concatenate([kf_recv[:, PER + cc, :] for cc in range(PER)], axis=0)
-    e_send[...] = skips.T[:8]
-    e_copies = to_peers(e_send, e_recv, e_send_sem, e_recv_sem)
+    gsig_ref[...] = (gather_channels(kf_recv) + skip_t * gradu_t[...]).T.astype(BF)
+    outs[1].start()
 
     pltpu.make_async_copy(f_recv, f_recv, f_recv_sem).wait()
     my_quarter = pl.ds(pl.multiple_of(dp * quarter, quarter), quarter)
@@ -551,19 +539,38 @@
         copy.start()
         h_copies.append(copy)
     pltpu.make_async_copy(h_send, h_recv.at[my_quarter, :], h_recv_sem).start()
-    gsig_ref[...] = (gather_channels(kf_recv) + skip_t * gradu_t[...]).T.astype(BF)
-    outs[1].start()
-
-    pltpu.make_async_copy(g_recv, g_recv, g_sem.at[1]).wait()
-    outs[3].start()
+
+    columns = [(zl == 0, ny)] + [
+        ((zl == 1) & (x == k), max(0, min(ny, extras - k * ny))) for k in range(nx)
+    ]
+
+    def block_copy(k, count):
+        rows_of = pl.ds(pl.multiple_of(column * g_size, g_size), count * g_size)
+        return pltpu.make_async_remote_copy(
+            src_ref=g_recv.at[rows_of, :], dst_ref=g_recv.at[rows_of, :],
+            send_sem=g_sem.at[2], recv_sem=g_sem.at[3],
+            device_id=(dp, member(lax.rem(g + k, group)), ch), device_id_type=MESH,
+        )
+
+    for here, count in columns:
+        if count:
+            @pl.when(here)
+            def _():
+                part = g_recv.at[pl.ds(0, count * g_size), :]
+                pltpu.make_async_copy(part, part, g_sem.at[1]).wait()
+                for k in range(1, group):
+                    block_copy(k, count).start()
 
     pltpu.make_async_copy(h_recv, h_recv, h_recv_sem).wait()
     gfilt_ref[...] = h_recv[...].astype(F32).T
     outs[2].start()
 
-    pltpu.make_async_copy(e_recv, e_recv, e_recv_sem).wait()
-    gskip_ref[...] = e_send[...] + e_recv[0] + e_recv[1] + e_recv[2]
-    outs[4].start()
+    for here, count in columns:
+        @pl.when(here)
+        def _():
+            part = g_recv.at[pl.ds(0, (n_own - count) * g_size), :]
+            pltpu.make_async_copy(part, part, g_sem.at[3]).wait()
+    outs[3].start()
 
     for sub in range(SUB):
         for qq in range(2):
@@ -582,7 +589,7 @@
     w_copy.wait_send()
     pre0_copy.wait_send()
     wf_copy.wait_send()
-    for copy in wy_copies + far_copies + pre_copies + ret_copies + f_copies + h_copies + e_copies:
+    for copy in wy_copies + far_copies + pre_copies + ret_copies + f_copies + h_copies:
         copy.wait_send()
 
     @pl.when(holds_far)
@@ -597,21 +604,24 @@
         part = b_send.at[:, pl.ds(0, count * LANES)]
         pltpu.make_async_copy(part, part, b_sem.at[0]).wait()
 
-    @pl.when(me < n_own)
+    @pl.when(is_owner)
     def _():
         b_sent(n_own - 1)
         for step in (1, 3, 2):
             q_copy(step).wait_send()
-
-        def sent(d, _):
+        for _ in range(1, ny):
             pltpu.make_async_copy(g_send, g_send, g_sem.at[0]).wait()
-            return 0
-
-        lax.fori_loop(1, n, sent, 0)
-
-    @pl.when(me >= n_own)
+
+    @pl.when(jnp.logical_not(is_owner))
     def _():
         b_sent(n_own)
+
+    for here, count in columns:
+        if count:
+            @pl.when(here)
+            def _():
+                for k in range(1, group):
+                    block_copy(k, count).wait_send()
 
     for out in outs:
         out.wait()
@@ -623,7 +633,8 @@
 
 
 def finish_kernel(
-    gsig_in, ggat_in, gfilt_in, gbank_in, gskip_in,
+    ny,
+    gsig_in, ggat_in, gfilt_in, gbank_in,
     gsig_out, ggat_out, gfilt_out, gskip_out, ga_out, gb_out,
     gsig_ref, ggat_ref, gfilt_ref, gbank_ref, gskip_ref, ga_ref, gb_ref, in_sem, out_sem,
 ):
@@ -631,11 +642,9 @@
     width = ga_ref.shape[2]
     g_size = 2 * max_rank
     up_chunks = half // LANES
+    nx = up_chunks // ny
     a_chunks = -(-width // LANES)
-    pairs = (
-        (gbank_in, gbank_ref), (gfilt_in, gfilt_ref), (gsig_in, gsig_ref), (ggat_in, ggat_ref),
-        (gskip_in.at[pl.ds(0, 1)], gskip_ref),
-    )
+    pairs = ((gbank_in, gbank_ref), (gfilt_in, gfilt_ref), (gsig_in, gsig_ref), (ggat_in, ggat_ref))
     loads = [pltpu.make_async_copy(s, d, in_sem.at[i]) for i, (s, d) in enumerate(pairs)]
     for load in loads:
         load.start()
@@ -645,17 +654,13 @@
     )
     stores = [pltpu.make_async_copy(s, d, out_sem.at[i]) for i, (s, d) in enumerate(pairs)]
     loads[0].wait()
-
-    def place(p, _):
-        block = gbank_ref[pl.ds(pl.multiple_of(p * g_size, g_size), g_size), :].astype(F32)
-        where = pl.ds(pl.multiple_of(p * LANES, LANES), LANES)
-        gb_ref[0, :, where] = block[:max_rank]
-        gb_ref[1, :, where] = block[max_rank:]
-        return 0
-
-    lax.fori_loop(0, up_chunks, place, 0, unroll=4)
+    for p in range(up_chunks):
+        at = ((p % nx) * ny + p // nx) * g_size
+        block = gbank_ref[at:at + g_size, :].astype(F32)
+        gb_ref[0, :, p * LANES:(p + 1) * LANES] = block[:max_rank]
+        gb_ref[1, :, p * LANES:(p + 1) * LANES] = block[max_rank:]
     stores[0].start()
-    for k in range(1, 5):
+    for k in range(1, 4):
         loads[k].wait()
         stores[k].start()
     size = min(LANES, width)
@@ -664,6 +669,10 @@
         block = gbank_ref[at:at + g_size, :].astype(F32)
         ga_ref[0, :, k * size:(k + 1) * size] = block[:max_rank, :size]
         ga_ref[1, :, k * size:(k + 1) * size] = block[max_rank:, :size]
+        at = (up_chunks + a_chunks + k) * g_size
+        block = gbank_ref[at:at + g_size, :].astype(F32)
+        gskip_ref[:, k * size:(k + 1) * size] = (block[0:1] + block[max_rank:max_rank + 1])[:, :size]
+    stores[4].start()
     stores[5].start()
     for store in stores:
         store.wait()
@@ -679,7 +688,7 @@
     cols = output_projection.shape[1] // 2
     max_rank = adapter_up_bank.shape[1]
     a_chunks = -(-width // LANES)
-    n_own = half // LANES + a_chunks
+    n_own = half // LANES + 2 * a_chunks
     piece = LANES // SUB
     group = 2 * min(4, n // 2)
     far_cols = 2 * cols // group
@@ -695,7 +704,6 @@
     ]
     block = pltpu.VMEM((n, PER, LANES), F32)
     eight = pltpu.VMEM((8 * n, LANES), F32)
-    two = pltpu.VMEM((n, 2 * PER, LANES), F32)
     wide = pltpu.VMEM((width, LANES), F32)
     spec = pltpu.VMEM((PER * rows, 2 * LANES), F32)
     rank = pltpu.VMEM((max_rank, LANES), F32)
@@ -706,19 +714,17 @@
             jax.ShapeDtypeStruct((LANES, width), BF),
             jax.ShapeDtypeStruct((LANES, width), F32),
             jax.ShapeDtypeStruct((2 * max_rank * n_own, LANES), BF),
-            jax.ShapeDtypeStruct((8, width), F32),
         ),
         in_specs=[smem] * 3 + [hbm] * len(arrays),
-        out_specs=(hbm,) * 5,
+        out_specs=(hbm,) * 4,
         scratch_shapes=[
             pltpu.VMEM((LANES, width), BF),
             pltpu.VMEM((LANES, width), BF),
             pltpu.VMEM((LANES, width), F32),
-            pltpu.VMEM((8, width), F32),
         ] + [pltpu.VMEM(a.shape, a.dtype) for a in arrays] + [
             pltpu.VMEM((LANES, half), BF),
             wide, wide, wide, spec, spec, spec,
-            eight, eight, block, block, block, block, block, block, two, two,
+            eight, eight, block, block, block, block, block, block, block, block,
             pltpu.VMEM((LANES, cols), BF),
             pltpu.VMEM((SUB, 2, piece, cols), BF),
             pltpu.VMEM((group, LANES, far_cols), BF),
@@ -744,11 +750,9 @@
             wide,
             pltpu.VMEM((width // 4, LANES), BF),
             pltpu.VMEM((width, LANES), BF),
-            pltpu.VMEM((8, width), F32),
-            pltpu.VMEM((3, 8, width), F32),
-            dma((len(arrays),)), dma((5,)), dma((5,)), dma((5,)), dma((SUB, 4)), dma((SUB,)), dma((2,)), dma((2,)),
+            dma((len(arrays),)), dma((4,)), dma((5,)), dma((5,)), dma((SUB, 4)), dma((SUB,)), dma((2,)), dma((2,)),
             dma((2,)), dma((SUB,)), dma((SUB,)), dma((SUB, 4)), dma, dma((2,)), dma((2,)), dma((2,)),
-            dma((4,)), dma, dma((2,)), dma((4,)), dma, dma((4,)), dma,
+            dma((4,)), dma, dma((4,)), dma((4,)), dma,
             dma((4,)), dma, dma((2,)), dma((2,)), dma((8,)), dma, dma((group,)), dma,
         ],
         compiler_params=pltpu.CompilerParams(
@@ -756,7 +760,7 @@
         ),
     )(adapter_index, sequence_rank, real_length, *arrays)
     grad_signal, grad_gating, grad_filt, grad_skip, grad_a, grad_b = pl.pallas_call(
-        finish_kernel,
+        functools.partial(finish_kernel, n // group),
         out_shape=(
             jax.ShapeDtypeStruct((LANES, width), BF),
             jax.ShapeDtypeStruct((LANES, width), BF),
@@ -765,13 +769,13 @@
             jax.ShapeDtypeStruct((2, max_rank, width), F32),
             jax.ShapeDtypeStruct((2, max_rank, half), F32),
         ),
-        in_specs=[hbm] * 5,
+        in_specs=[hbm] * 4,
         out_specs=(hbm,) * 6,
         scratch_shapes=[
             pltpu.VMEM((LANES, width), BF), pltpu.VMEM((LANES, width), BF), pltpu.VMEM((LANES, width), F32),
             pltpu.VMEM((2 * max_rank * n_own, LANES), BF), pltpu.VMEM((1, width), F32),
             pltpu.VMEM((2, max_rank, width), F32), pltpu.VMEM((2, max_rank, half), F32),
-            dma((5,)), dma((6,)),
+            dma((4,)), dma((6,)),
         ],
         compiler_params=pltpu.CompilerParams(vmem_limit_bytes=VMEM_LIMIT),
     )(*outs)

time: 88.4 us -> 83.5 us (0.945)
  Pallas kernels: 85.6 us -> 80.8 us
    pallas_call x1, Pallas kernels: 83.5 us -> 78.8 us  [local(): pl.pallas_call(functools.partial(kernel, n), out_shape=(jax.ShapeDtypeStr...]
where the time goes in v4:
time: 83.5 us; the launch traced here: 83.3 us
  Pallas kernels  80.8 us (97%)
  between operations  2.58 us (3%)
    pallas_call x1, Pallas kernels, local(): pl.pallas_call(functools.partial(kernel, n), out_shape=(jax.ShapeDtypeStr...  78.8 us
    pallas_call x1, Pallas kernels, local(): pl.pallas_call(functools.partial(finish_kernel, n // group), out_shape=(j...  1.96 us

profile of v4, /device:TPU:6, one launch (start us, length us, event | category | flops | bytes accessed | tf_op | source)
XLA Modules:
  0.0 83.3 jit_solution(16384770761780296241)
XLA Ops:
  2.6 78.8 %shard_map.208 = (bf16[128,256]{1,0:T(8,128)(2,1)}, bf16[128,256]{1,0:T(8,128)(2,1)}, f32[128,256]{1,0:T(8,128)}, bf16[1152,128]{1,0:T(8,128)(2,1)}) custom-call(s32[1]{0:T(128)S(6)} %copy.23.index_ref, s32[1]{0:T(128)S(6)} %copy.24.rank_ref, s32[1]{0:T(128)S(6)} %copy.25.length_ref, bf16[128,256]{1,0:T(8,128)(2,1)} %bitcast.10, bf16[128,256]{1,0:T(8,128)(2,1)} %bitcast.11, ...), custom_call_target="tpu_custom_call" | custom-call | tf_op jit(solution)/shard_map/pallas_call | solution.py:710
  81.4 2.0 %shard_map.209 = (bf16[128,256]{1,0:T(8,128)(2,1)}, bf16[128,256]{1,0:T(8,128)(2,1)}, f32[128,256]{1,0:T(8,128)}, f32[1,256]{1,0:T(1,128)}, f32[2,16,256]{2,1,0:T(8,128)}, /*index=5*/f32[2,16,4096]{2,1,0:T(8,128)}) custom-call(bf16[128,256]{1,0:T(8,128)(2,1)} %get-tuple-element.16.gsig_in, bf16[128,256]{1,0:T(8,128)(2,1)} %get-tuple-element.17.ggat_in, ...), custom_call_target="tpu_custom_call" | custom-call | tf_op jit(solution)/shard_map/pallas_call | solution.py:762

commit v5 on v4

--- a/solution.py
+++ b/solution.py
@@ -81,6 +81,7 @@
     t1_ref, t2_ref, t2b_ref, t1b_ref, tc_ref, ts_ref,
     masked, sig_t, gate_t, gradu_t, spec_s, spec_f, spec_g,
     sf_send, sf_recv, c_send, c_recv, u_send, u_recv, ks_send, ks_recv, kf_send, kf_recv,
+    u_stage, u_back, ks_stage, ks_back, kf_stage, kf_back,
     m_own, m_recv, m_far, w_far, far_send, far_recv, w_recv, pre0_send, pre0_recv, pre_send, pre_recv, ret_send, ret_recv,
     d_send, d_recv, r_send, r_recv,
     b_send, b_recv, q_send, q_recv, g_send, g_recv, f_send, f_recv, corr_st, h_send, h_recv,
@@ -114,6 +115,16 @@
     rows = t1_ref.shape[0] // 2
     a_chunks = -(-width // LANES)
 
+    pairs = (
+        (signal_hbm, signal_ref), (filt_hbm, filt_ref), (cot_hbm, cot_ref), (up_hbm, up_ref),
+        (w_hbm, w_ref), (t1_hbm, t1_ref), (t2_hbm, t2_ref), (t2b_hbm, t2b_ref), (t1b_hbm, t1b_ref),
+        (tc_hbm, tc_ref), (ts_hbm, ts_ref), (gating_hbm, gating_ref), (down_hbm, down_ref),
+        (skip_hbm, skip_ref),
+    )
+    loads = [pltpu.make_async_copy(s, d, in_sem.at[i]) for i, (s, d) in enumerate(pairs)]
+    for load in loads:
+        load.start()
+
     barrier = pltpu.get_barrier_semaphore()
     for d in range(4):
         for z in range(2):
@@ -138,16 +149,6 @@
                 barrier, inc=1, device_id=(dp, member(z * nx + lax.rem(x + k, nx)), other),
                 device_id_type=MESH,
             )
-
-    pairs = (
-        (signal_hbm, signal_ref), (filt_hbm, filt_ref), (cot_hbm, cot_ref), (up_hbm, up_ref),
-        (w_hbm, w_ref), (t1_hbm, t1_ref), (t2_hbm, t2_ref), (t2b_hbm, t2b_ref), (t1b_hbm, t1b_ref),
-        (tc_hbm, tc_ref), (ts_hbm, ts_ref), (gating_hbm, gating_ref), (down_hbm, down_ref),
-        (skip_hbm, skip_ref),
-    )
-    loads = [pltpu.make_async_copy(s, d, in_sem.at[i]) for i, (s, d) in enumerate(pairs)]
-    for load in loads:
-        load.start()
 
     loads[0].wait()
     loads[1].wait()
@@ -416,7 +417,8 @@
     grad_u = grad_y * gate_t[...]
     gradu_t[...] = grad_u
     for cc in range(PER):
-        u_send[:, cc, :] = gradu_t[cc * n:(cc + 1) * n, :]
+        u_stage[:, cc, :] = gradu_t[cc * n:(cc + 1) * n, :]
+    u_send[...] = u_stage[...].astype(BF)
     a2a_start(2, u_send, u_recv, block)
     r_copy.wait()
     fwd_rank = (2.0 * (r_send[...] + r_recv[...]) * keep).astype(BF)
@@ -463,13 +465,16 @@
     outs[0].start()
 
     a2a_wait(2, u_recv)
-    forward(lambda cc: u_recv[:, cc, :], spec_g)
+    u_back[...] = u_recv[...].astype(F32)
+    forward(lambda cc: u_back[:, cc, :], spec_g)
     g_re, g_im = spec_g[:, :LANES], spec_g[:, LANES:]
     s_re, s_im = spec_s[:, :LANES], spec_s[:, LANES:]
-    spread_channels(ks_send, inverse(g_re * s_re + g_im * s_im, g_im * s_re - g_re * s_im))
+    spread_channels(ks_stage, inverse(g_re * s_re + g_im * s_im, g_im * s_re - g_re * s_im))
+    ks_send[...] = ks_stage[...].astype(BF)
     a2a_start(3, ks_send, ks_recv, block)
     f_re, f_im = spec_f[:, :LANES], spec_f[:, LANES:]
-    spread_channels(kf_send, inverse(g_re * f_re + g_im * f_im, g_im * f_re - g_re * f_im))
+    spread_channels(kf_stage, inverse(g_re * f_re + g_im * f_im, g_im * f_re - g_re * f_im))
+    kf_send[...] = kf_stage[...].astype(BF)
     a2a_start(4, kf_send, kf_recv, block)
 
     column = zl * plane + x * ny
@@ -493,7 +498,8 @@
 
     a2a_wait(3, ks_recv)
     quarter = width // 4
-    corr_st[...] = gather_channels(ks_recv)
+    ks_back[...] = ks_recv[...].astype(F32)
+    corr_st[...] = gather_channels(ks_back)
     f_send[...] = corr_st[...].astype(BF)
     f_copies = []
     for step in (1, 3, 2):
@@ -521,7 +527,8 @@
         pltpu.make_async_copy(g_send, g_recv.at[bank_rows, :], g_sem.at[1]).start()
 
     a2a_wait(4, kf_recv)
-    gsig_ref[...] = (gather_channels(kf_recv) + skip_t * gradu_t[...]).T.astype(BF)
+    kf_back[...] = kf_recv[...].astype(F32)
+    gsig_ref[...] = (gather_channels(kf_back) + skip_t * gradu_t[...]).T.astype(BF)
     outs[1].start()
 
     pltpu.make_async_copy(f_recv, f_recv, f_recv_sem).wait()
@@ -703,6 +710,7 @@
         jnp.swapaxes(adapter_down_bank, 1, 2), adapter_up_bank, *consts,
     ]
     block = pltpu.VMEM((n, PER, LANES), F32)
+    narrow = pltpu.VMEM((n, PER, LANES), BF)
     eight = pltpu.VMEM((8 * n, LANES), F32)
     wide = pltpu.VMEM((width, LANES), F32)
     spec = pltpu.VMEM((PER * rows, 2 * LANES), F32)
@@ -724,7 +732,8 @@
         ] + [pltpu.VMEM(a.shape, a.dtype) for a in arrays] + [
             pltpu.VMEM((LANES, half), BF),
             wide, wide, wide, spec, spec, spec,
-            eight, eight, block, block, block, block, block, block, block, block,
+            eight, eight, block, block, narrow, narrow, narrow, narrow, narrow, narrow,
+            block, block, block, block, block, block,
             pltpu.VMEM((LANES, cols), BF),
             pltpu.VMEM((SUB, 2, piece, cols), BF),
             pltpu.VMEM((group, LANES, far_cols), BF),

time: 83.5 us -> 80.4 us (0.963)
  Pallas kernels: 80.8 us -> 77.2 us
    pallas_call x1, Pallas kernels: 78.8 us -> 75.2 us  [local(): pl.pallas_call(functools.partial(kernel, n), out_shape=(jax.ShapeDtypeStr...]
where the time goes in v5:
time: 80.4 us; the launch traced here: 79.8 us
  Pallas kernels  77.2 us (96%)
  between operations  2.58 us (3%)
    pallas_call x1, Pallas kernels, local(): pl.pallas_call(functools.partial(kernel, n), out_shape=(jax.ShapeDtypeStr...  75.2 us
    pallas_call x1, Pallas kernels, local(): pl.pallas_call(functools.partial(finish_kernel, n // group), out_shape=(j...  1.96 us

profile of v5, /device:TPU:6, one launch (start us, length us, event | category | flops | bytes accessed | tf_op | source)
XLA Modules:
  0.0 79.8 jit_solution(1939744739003913873)
XLA Ops:
  2.6 75.2 %shard_map.208 = (bf16[128,256]{1,0:T(8,128)(2,1)}, bf16[128,256]{1,0:T(8,128)(2,1)}, f32[128,256]{1,0:T(8,128)}, bf16[1152,128]{1,0:T(8,128)(2,1)}) custom-call(s32[1]{0:T(128)S(6)} %copy.23.index_ref, s32[1]{0:T(128)S(6)} %copy.24.rank_ref, s32[1]{0:T(128)S(6)} %copy.25.length_ref, bf16[128,256]{1,0:T(8,128)(2,1)} %bitcast.10, bf16[128,256]{1,0:T(8,128)(2,1)} %bitcast.11, ...), custom_call_target="tpu_custom_call" | custom-call | tf_op jit(solution)/shard_map/pallas_call | solution.py:718
  77.8 2.0 %shard_map.209 = (bf16[128,256]{1,0:T(8,128)(2,1)}, bf16[128,256]{1,0:T(8,128)(2,1)}, f32[128,256]{1,0:T(8,128)}, f32[1,256]{1,0:T(1,128)}, f32[2,16,256]{2,1,0:T(8,128)}, /*index=5*/f32[2,16,4096]{2,1,0:T(8,128)}) custom-call(bf16[128,256]{1,0:T(8,128)(2,1)} %get-tuple-element.16.gsig_in, bf16[128,256]{1,0:T(8,128)(2,1)} %get-tuple-element.17.ggat_in, ...), custom_call_target="tpu_custom_call" | custom-call | tf_op jit(solution)/shard_map/pallas_call | solution.py:771

commit v6 on v5

--- a/solution.py
+++ b/solution.py
@@ -96,8 +96,8 @@
     other = 1 - ch
     plane = n // 2
     zl, spot = lax.div(me, plane), lax.rem(me, plane)
-    group = m_far.shape[0]
-    nx = group // 2
+    nx = m_far.shape[0]
+    group = 2 * nx
     ny = plane // nx
     y, x = lax.div(spot, nx), lax.rem(spot, nx)
     g = zl * nx + x
@@ -243,28 +243,28 @@
     my_slice = pl.ds(pl.multiple_of(y * slice_rows, slice_rows), slice_rows)
 
     wf_copy = pltpu.make_async_remote_copy(
-        src_ref=w_hbm.at[my_slice, pl.ds(pl.multiple_of(g * far_cols, far_cols), far_cols)],
+        src_ref=w_hbm.at[my_slice, pl.ds(pl.multiple_of(x * far_cols, far_cols), far_cols)],
         dst_ref=w_far.at[my_slice, :],
         send_sem=wf_sem.at[0], recv_sem=wf_sem.at[1], device_id=(far, me, ch), device_id_type=MESH,
     )
     wf_copy.start()
 
     def far_copy(d, c):
-        k = lax.rem(g + d, group)
+        k = lax.rem(x + d, nx)
         at = lax.rem(far, 2) * 2 * cols + k * far_cols
         src = cot_hbm.at[:, pl.ds(pl.multiple_of(at, far_cols), far_cols)]
         if d == 0 and c == 0:
             return pltpu.make_async_copy(src, m_far.at[d], far_sem.at[1])
         return pltpu.make_async_remote_copy(
             src_ref=src, dst_ref=m_far.at[d], send_sem=far_sem.at[0], recv_sem=far_sem.at[1],
-            device_id=(dp, member(k), lax.rem(ch + c, 2)), device_id_type=MESH,
+            device_id=(dp, member(zl * nx + k), lax.rem(ch + c, 2)), device_id_type=MESH,
         )
 
     holds_far = ch == lax.div(far, 2)
 
     @pl.when(holds_far)
     def _():
-        for d in range(group):
+        for d in range(nx):
             for c in range(2):
                 far_copy(d, c).start()
 
@@ -378,15 +378,15 @@
     if ny > 1:
         rest = w_far.at[pl.ds(0, (ny - 1) * slice_rows), :]
         pltpu.make_async_copy(rest, rest, wy_recv_sem).wait()
-    far_part = dot_t(m_far[...].reshape(group * LANES, far_cols), w_far[...])
+    far_part = dot_t(m_far[...].reshape(nx * LANES, far_cols), w_far[...])
     far_send[...] = far_part[LANES:].astype(BF)
     own_part = own_part + far_part[:LANES]
     far_copies = []
-    for d in range(1, group):
+    for d in range(1, nx):
         copy = pltpu.make_async_remote_copy(
             src_ref=far_send.at[pl.ds((d - 1) * LANES, LANES), :], dst_ref=far_recv.at[d - 1],
             send_sem=fr_send_sem.at[d], recv_sem=fr_recv_sem,
-            device_id=(dp, member(lax.rem(g + group - d, group)), ch), device_id_type=MESH,
+            device_id=(dp, member(zl * nx + lax.rem(x + nx - d, nx)), ch), device_id_type=MESH,
         )
         copy.start()
         far_copies.append(copy)
@@ -411,7 +411,7 @@
     pltpu.make_async_copy(far_recv, far_recv, fr_recv_sem).wait()
     for k in range(2):
         grad_y = grad_y + ret_recv[k].astype(F32)
-    for k in range(group - 1):
+    for k in range(nx - 1):
         grad_y = grad_y + far_recv[k].astype(F32)
     grad_y = grad_y.T * live_row + dot_0(down_sel, back_rank)
     grad_u = grad_y * gate_t[...]
@@ -472,10 +472,6 @@
     spread_channels(ks_stage, inverse(g_re * s_re + g_im * s_im, g_im * s_re - g_re * s_im))
     ks_send[...] = ks_stage[...].astype(BF)
     a2a_start(3, ks_send, ks_recv, block)
-    f_re, f_im = spec_f[:, :LANES], spec_f[:, LANES:]
-    spread_channels(kf_stage, inverse(g_re * f_re + g_im * f_im, g_im * f_re - g_re * f_im))
-    kf_send[...] = kf_stage[...].astype(BF)
-    a2a_start(4, kf_send, kf_recv, block)
 
     column = zl * plane + x * ny
     is_owner = column + y < n_own
@@ -495,6 +491,25 @@
         q_send[...] = jnp.concatenate([acc * pick0, acc * pick1], axis=0)
         for step in (1, 3, 2):
             q_copy(step).start()
+
+    f_re, f_im = spec_f[:, :LANES], spec_f[:, LANES:]
+    spread_channels(kf_stage, inverse(g_re * f_re + g_im * f_im, g_im * f_re - g_re * f_im))
+    kf_send[...] = kf_stage[...].astype(BF)
+    a2a_start(4, kf_send, kf_recv, block)
+
+    g_size = 2 * max_rank
+    bank_rows = pl.ds(pl.multiple_of((column + y) * g_size, g_size), g_size)
+
+    @pl.when(is_owner)
+    def _():
+        pltpu.make_async_copy(q_recv, q_recv, q_recv_sem).wait()
+        g_send[...] = (q_send[...] + q_recv[0] + q_recv[1] + q_recv[2]).astype(BF)
+        for k in range(1, ny):
+            pltpu.make_async_remote_copy(
+                src_ref=g_send, dst_ref=g_recv.at[bank_rows, :], send_sem=g_sem.at[0], recv_sem=g_sem.at[1],
+                device_id=(dp, zl * plane + lax.rem(y + k, ny) * nx + x, ch), device_id_type=MESH,
+            ).start()
+        pltpu.make_async_copy(g_send, g_recv.at[bank_rows, :], g_sem.at[1]).start()
 
     a2a_wait(3, ks_recv)
     quarter = width // 4
@@ -512,19 +527,26 @@
         copy.start()
         f_copies.append(copy)
 
-    g_size = 2 * max_rank
-    bank_rows = pl.ds(pl.multiple_of((column + y) * g_size, g_size), g_size)
-
-    @pl.when(is_owner)
-    def _():
-        pltpu.make_async_copy(q_recv, q_recv, q_recv_sem).wait()
-        g_send[...] = (q_send[...] + q_recv[0] + q_recv[1] + q_recv[2]).astype(BF)
-        for k in range(1, ny):
-            pltpu.make_async_remote_copy(
-                src_ref=g_send, dst_ref=g_recv.at[bank_rows, :], send_sem=g_sem.at[0], recv_sem=g_sem.at[1],
-                device_id=(dp, zl * plane + lax.rem(y + k, ny) * nx + x, ch), device_id_type=MESH,
-            ).start()
-        pltpu.make_async_copy(g_send, g_recv.at[bank_rows, :], g_sem.at[1]).start()
+    columns = [(zl == 0, ny)] + [
+        ((zl == 1) & (x == k), max(0, min(ny, extras - k * ny))) for k in range(nx)
+    ]
+
+    def block_copy(k, count):
+        rows_of = pl.ds(pl.multiple_of(column * g_size, g_size), count * g_size)
+        return pltpu.make_async_remote_copy(
+            src_ref=g_recv.at[rows_of, :], dst_ref=g_recv.at[rows_of, :],
+            send_sem=g_sem.at[2], recv_sem=g_sem.at[3],
+            device_id=(dp, member(lax.rem(g + k, group)), ch), device_id_type=MESH,
+        )
+
+    for here, count in columns:
+        if count:
+            @pl.when(here)
+            def _():
+                part = g_recv.at[pl.ds(0, count * g_size), :]
+                pltpu.make_async_copy(part, part, g_sem.at[1]).wait()
+                for k in range(1, group):
+                    block_copy(k, count).start()
 
     a2a_wait(4, kf_recv)
     kf_back[...] = kf_recv[...].astype(F32)
@@ -546,27 +568,6 @@
         copy.start()
         h_copies.append(copy)
     pltpu.make_async_copy(h_send, h_recv.at[my_quarter, :], h_recv_sem).start()
-
-    columns = [(zl == 0, ny)] + [
-        ((zl == 1) & (x == k), max(0, min(ny, extras - k * ny))) for k in range(nx)
-    ]
-
-    def block_copy(k, count):
-        rows_of = pl.ds(pl.multiple_of(column * g_size, g_size), count * g_size)
-        return pltpu.make_async_remote_copy(
-            src_ref=g_recv.at[rows_of, :], dst_ref=g_recv.at[rows_of, :],
-            send_sem=g_sem.at[2], recv_sem=g_sem.at[3],
-            device_id=(dp, member(lax.rem(g + k, group)), ch), device_id_type=MESH,
-        )
-
-    for here, count in columns:
-        if count:
-            @pl.when(here)
-            def _():
-                part = g_recv.at[pl.ds(0, count * g_size), :]
-                pltpu.make_async_copy(part, part, g_sem.at[1]).wait()
-                for k in range(1, group):
-                    block_copy(k, count).start()
 
     pltpu.make_async_copy(h_recv, h_recv, h_recv_sem).wait()
     gfilt_ref[...] = h_recv[...].astype(F32).T
@@ -605,7 +606,7 @@
             pltpu.make_async_copy(m_far.at[0], m_far.at[0], far_sem.at[0]).wait()
             return 0
 
-        lax.fori_loop(1, 2 * group, sent, 0)
+        lax.fori_loop(1, 2 * nx, sent, 0)
 
     def b_sent(count):
         part = b_send.at[:, pl.ds(0, count * LANES)]
@@ -697,8 +698,8 @@
     a_chunks = -(-width // LANES)
     n_own = half // LANES + 2 * a_chunks
     piece = LANES // SUB
-    group = 2 * min(4, n // 2)
-    far_cols = 2 * cols // group
+    nx = min(4, n // 2)
+    far_cols = 2 * cols // nx
     consts = [jnp.asarray(t) for t in tables(n)]
     rows = consts[4].shape[0]
     vmem = pl.BlockSpec(memory_space=pltpu.VMEM)
@@ -736,10 +737,10 @@
             block, block, block, block, block, block,
             pltpu.VMEM((LANES, cols), BF),
             pltpu.VMEM((SUB, 2, piece, cols), BF),
-            pltpu.VMEM((group, LANES, far_cols), BF),
+            pltpu.VMEM((nx, LANES, far_cols), BF),
             pltpu.VMEM((width, far_cols), BF),
-            pltpu.VMEM(((group - 1) * LANES, width), BF),
-            pltpu.VMEM((group - 1, LANES, width), BF),
+            pltpu.VMEM(((nx - 1) * LANES, width), BF),
+            pltpu.VMEM((nx - 1, LANES, width), BF),
             pltpu.VMEM((width, cols), BF),
             pltpu.VMEM((LANES, width), BF),
             pltpu.VMEM((LANES, width), BF),
@@ -762,14 +763,14 @@
             dma((len(arrays),)), dma((4,)), dma((5,)), dma((5,)), dma((SUB, 4)), dma((SUB,)), dma((2,)), dma((2,)),
             dma((2,)), dma((SUB,)), dma((SUB,)), dma((SUB, 4)), dma, dma((2,)), dma((2,)), dma((2,)),
             dma((4,)), dma, dma((4,)), dma((4,)), dma,
-            dma((4,)), dma, dma((2,)), dma((2,)), dma((8,)), dma, dma((group,)), dma,
+            dma((4,)), dma, dma((2,)), dma((2,)), dma((8,)), dma, dma((nx,)), dma,
         ],
         compiler_params=pltpu.CompilerParams(
             collective_id=0, has_side_effects=True, vmem_limit_bytes=VMEM_LIMIT
         ),
     )(adapter_index, sequence_rank, real_length, *arrays)
     grad_signal, grad_gating, grad_filt, grad_skip, grad_a, grad_b = pl.pallas_call(
-        functools.partial(finish_kernel, n // group),
+        functools.partial(finish_kernel, n // (2 * nx)),
         out_shape=(
             jax.ShapeDtypeStruct((LANES, width), BF),
             jax.ShapeDtypeStruct((LANES, width), BF),

time: 80.4 us -> 79.5 us (0.989)
  Pallas kernels: 77.2 us -> 76 us
    pallas_call x1, Pallas kernels: 75.2 us -> 74 us  [local(): pl.pallas_call(functools.partial(kernel, n), out_shape=(jax.ShapeDtypeStr...]
where the time goes in v6:
time: 79.5 us; the launch traced here: 78.6 us
  Pallas kernels  76 us (96%)
  between operations  2.58 us (3%)
    pallas_call x1, Pallas kernels, local(): pl.pallas_call(functools.partial(kernel, n), out_shape=(jax.ShapeDtypeStr...  74 us
    pallas_call x1, Pallas kernels, local(): pl.pallas_call(functools.partial(finish_kernel, n // (2 * nx)), out_shape...  1.96 us

profile of v6, /device:TPU:6, one launch (start us, length us, event | category | flops | bytes accessed | tf_op | source)
XLA Modules:
  0.0 78.6 jit_solution(13473107990349074672)
XLA Ops:
  2.6 74.0 %shard_map.208 = (bf16[128,256]{1,0:T(8,128)(2,1)}, bf16[128,256]{1,0:T(8,128)(2,1)}, f32[128,256]{1,0:T(8,128)}, bf16[1152,128]{1,0:T(8,128)(2,1)}) custom-call(s32[1]{0:T(128)S(6)} %copy.23.index_ref, s32[1]{0:T(128)S(6)} %copy.24.rank_ref, s32[1]{0:T(128)S(6)} %copy.25.length_ref, bf16[128,256]{1,0:T(8,128)(2,1)} %bitcast.10, bf16[128,256]{1,0:T(8,128)(2,1)} %bitcast.11, ...), custom_call_target="tpu_custom_call" | custom-call | tf_op jit(solution)/shard_map/pallas_call | solution.py:719
  76.6 2.0 %shard_map.209 = (bf16[128,256]{1,0:T(8,128)(2,1)}, bf16[128,256]{1,0:T(8,128)(2,1)}, f32[128,256]{1,0:T(8,128)}, f32[1,256]{1,0:T(1,128)}, f32[2,16,256]{2,1,0:T(8,128)}, /*index=5*/f32[2,16,4096]{2,1,0:T(8,128)}) custom-call(bf16[128,256]{1,0:T(8,128)(2,1)} %get-tuple-element.16.gsig_in, bf16[128,256]{1,0:T(8,128)(2,1)} %get-tuple-element.17.ggat_in, ...), custom_call_target="tpu_custom_call" | custom-call | tf_op jit(solution)/shard_map/pallas_call | solution.py:772

commit v7 on v6

--- a/solution.py
+++ b/solution.py
@@ -94,6 +94,8 @@
     me = lax.axis_index("seq")
     ch = lax.axis_index("chan")
     other = 1 - ch
+    width = w_ref.shape[0]
+    cols = w_ref.shape[1] // 2
     plane = n // 2
     zl, spot = lax.div(me, plane), lax.rem(me, plane)
     nx = m_far.shape[0]
@@ -101,13 +103,13 @@
     ny = plane // nx
     y, x = lax.div(spot, nx), lax.rem(spot, nx)
     g = zl * nx + x
-    far_cols = m_far.shape[2]
+    far_cols = 2 * cols // nx
+    near_cols = m_recv.shape[3]
+    shared_cols = (2 * cols - 2 * near_cols) // nx
 
     def member(k):
         return lax.div(k, nx) * plane + y * nx + lax.rem(k, nx)
 
-    width = w_ref.shape[0]
-    cols = w_ref.shape[1] // 2
     half = cot_ref.shape[1]
     piece = LANES // SUB
     n_own = b_send.shape[1] // LANES
@@ -199,7 +201,7 @@
     def cot_copy(sub, qq, hh):
         q = 2 * ch + qq
         return pltpu.make_async_remote_copy(
-            src_ref=cot_hbm.at[pl.ds(sub * piece, piece), pl.ds((2 * qq + hh) * cols, cols)],
+            src_ref=cot_hbm.at[pl.ds(sub * piece, piece), pl.ds(2 * qq * cols + hh * near_cols, near_cols)],
             dst_ref=m_recv.at[sub, zl],
             send_sem=m_send_sem.at[sub, 2 * qq + hh],
             recv_sem=m_recv_sem.at[sub],
@@ -242,23 +244,46 @@
     slice_rows = width // ny
     my_slice = pl.ds(pl.multiple_of(y * slice_rows, slice_rows), slice_rows)
 
-    wf_copy = pltpu.make_async_remote_copy(
-        src_ref=w_hbm.at[my_slice, pl.ds(pl.multiple_of(x * far_cols, far_cols), far_cols)],
-        dst_ref=w_far.at[my_slice, :],
-        send_sem=wf_sem.at[0], recv_sem=wf_sem.at[1], device_id=(far, me, ch), device_id_type=MESH,
-    )
-    wf_copy.start()
+    wf_copies = []
+    for i, (b, first, size, at) in enumerate((
+        (2, 0, far_cols, 0),
+        (3, 2 * near_cols, shared_cols, far_cols),
+        (1, 2 * near_cols, shared_cols, far_cols + shared_cols),
+    )):
+        wf_copies.append(pltpu.make_async_remote_copy(
+            src_ref=w_hbm.at[my_slice, pl.ds(pl.multiple_of(first + x * size, size), size)],
+            dst_ref=w_far.at[my_slice, pl.ds(at, size)],
+            send_sem=wf_sem.at[2 * i], recv_sem=wf_sem.at[2 * i + 1],
+            device_id=(lax.rem(dp + b, 4), me, ch), device_id_type=MESH,
+        ))
+        wf_copies[-1].start()
+
+    def row_copy(src, at, size, d, c, send_sem):
+        dst = m_far.at[d, :, pl.ds(at, size)]
+        if d == 0 and c == 0:
+            return pltpu.make_async_copy(src, dst, far_sem.at[1])
+        return pltpu.make_async_remote_copy(
+            src_ref=src, dst_ref=dst, send_sem=send_sem, recv_sem=far_sem.at[1],
+            device_id=(dp, member(zl * nx + lax.rem(x + d, nx)), lax.rem(ch + c, 2)), device_id_type=MESH,
+        )
 
     def far_copy(d, c):
-        k = lax.rem(x + d, nx)
-        at = lax.rem(far, 2) * 2 * cols + k * far_cols
+        at = lax.rem(far, 2) * 2 * cols + lax.rem(x + d, nx) * far_cols
         src = cot_hbm.at[:, pl.ds(pl.multiple_of(at, far_cols), far_cols)]
-        if d == 0 and c == 0:
-            return pltpu.make_async_copy(src, m_far.at[d], far_sem.at[1])
-        return pltpu.make_async_remote_copy(
-            src_ref=src, dst_ref=m_far.at[d], send_sem=far_sem.at[0], recv_sem=far_sem.at[1],
-            device_id=(dp, member(zl * nx + k), lax.rem(ch + c, 2)), device_id_type=MESH,
-        )
+        return row_copy(src, 0, far_cols, d, c, far_sem.at[0])
+
+    def shared_copy(qq, step, d, c):
+        at = 2 * qq * cols + 2 * near_cols + lax.rem(x + d, nx) * shared_cols
+        src = cot_hbm.at[:, pl.ds(pl.multiple_of(at, shared_cols), shared_cols)]
+        return row_copy(src, far_cols + (step // 3) * shared_cols, shared_cols, d, c, far_sem.at[2])
+
+    for qq in range(2):
+        for step in (1, 3):
+            @pl.when(lax.rem(2 * ch + qq - dp + 4, 4) == step)
+            def _():
+                for d in range(nx):
+                    for c in range(2):
+                        shared_copy(qq, step, d, c).start()
 
     holds_far = ch == lax.div(far, 2)
 
@@ -275,11 +300,12 @@
         )
 
     w_copy = to_chan(
-        w_hbm.at[:, pl.ds(pl.multiple_of(other * cols, LANES), cols)], w_recv, w_sem.at[0], w_sem.at[1]
+        w_hbm.at[:, pl.ds(pl.multiple_of(other * near_cols, LANES), w_recv.shape[1])], w_recv, w_sem.at[0], w_sem.at[1]
     )
     w_copy.start()
 
-    wf_copy.wait_recv()
+    for copy in wf_copies:
+        copy.wait_recv()
     wy_copies = []
     for k in range(1, ny):
         copy = pltpu.make_async_remote_copy(
@@ -306,7 +332,8 @@
     own_cols = pl.ds(pl.multiple_of(ch * cols, LANES), cols)
     pltpu.make_async_copy(m_own, m_own, own_sem.at[1]).wait()
     w_copy.wait_recv()
-    pre0_send[...] = dot_t(m_own[...], w_recv[...]).astype(BF)
+    skipped = pl.ds(pl.multiple_of(ch * (cols - near_cols), LANES), cols)
+    pre0_send[...] = dot_t(m_own[...], w_recv[:, skipped]).astype(BF)
     pre0_copy = to_chan(pre0_send, pre0_recv, pre0_sem.at[0], pre0_sem.at[1])
     pre0_copy.start()
     own_part = dot_t(m_own[...], w_ref[:, own_cols])
@@ -315,12 +342,12 @@
 
     def project(sub):
         pltpu.make_async_copy(m_recv.at[sub], m_recv.at[sub], m_recv_sem.at[sub]).wait()
-        part = m_recv[sub].reshape(2 * piece, cols)
-        pre_send[sub] = dot_t(part, w_recv[...]).astype(BF)
+        part = m_recv[sub].reshape(2 * piece, near_cols)
+        pre_send[sub] = dot_t(part, w_recv[:, :near_cols]).astype(BF)
         copy = to_chan(pre_send.at[sub], pre_recv.at[sub], pre_send_sem.at[sub], pre_recv_sem.at[sub])
         copy.start()
         pre_copies.append(copy)
-        return dot_t(part, w_ref[:, own_cols])
+        return dot_t(part, w_ref[:, pl.ds(pl.multiple_of(ch * near_cols, LANES), near_cols)])
 
     def give_back(sub, mine):
         pre_copies[sub].wait_recv()
@@ -378,7 +405,7 @@
     if ny > 1:
         rest = w_far.at[pl.ds(0, (ny - 1) * slice_rows), :]
         pltpu.make_async_copy(rest, rest, wy_recv_sem).wait()
-    far_part = dot_t(m_far[...].reshape(nx * LANES, far_cols), w_far[...])
+    far_part = dot_t(m_far[...].reshape(nx * LANES, far_cols + 2 * shared_cols), w_far[...])
     far_send[...] = far_part[LANES:].astype(BF)
     own_part = own_part + far_part[:LANES]
     far_copies = []
@@ -596,14 +623,21 @@
         a2a_wait_send(k, src, 1)
     w_copy.wait_send()
     pre0_copy.wait_send()
-    wf_copy.wait_send()
-    for copy in wy_copies + far_copies + pre_copies + ret_copies + f_copies + h_copies:
+    for copy in wf_copies + wy_copies + far_copies + pre_copies + ret_copies + f_copies + h_copies:
         copy.wait_send()
+
+    def shared_sent(d, _):
+        part = m_far.at[0, :, pl.ds(far_cols, shared_cols)]
+        pltpu.make_async_copy(part, part, far_sem.at[2]).wait()
+        return 0
+
+    lax.fori_loop(1, 2 * nx, shared_sent, 0)
 
     @pl.when(holds_far)
     def _():
         def sent(d, _):
-            pltpu.make_async_copy(m_far.at[0], m_far.at[0], far_sem.at[0]).wait()
+            part = m_far.at[0, :, pl.ds(0, far_cols)]
+            pltpu.make_async_copy(part, part, far_sem.at[0]).wait()
             return 0
 
         lax.fori_loop(1, 2 * nx, sent, 0)
@@ -699,7 +733,9 @@
     n_own = half // LANES + 2 * a_chunks
     piece = LANES // SUB
     nx = min(4, n // 2)
-    far_cols = 2 * cols // nx
+    shared = cols // 2
+    near_cols = cols - shared // 2
+    row_cols = 2 * (cols + shared) // nx
     consts = [jnp.asarray(t) for t in tables(n)]
     rows = consts[4].shape[0]
     vmem = pl.BlockSpec(memory_space=pltpu.VMEM)
@@ -736,12 +772,12 @@
             eight, eight, block, block, narrow, narrow, narrow, narrow, narrow, narrow,
             block, block, block, block, block, block,
             pltpu.VMEM((LANES, cols), BF),
-            pltpu.VMEM((SUB, 2, piece, cols), BF),
-            pltpu.VMEM((nx, LANES, far_cols), BF),
-            pltpu.VMEM((width, far_cols), BF),
+            pltpu.VMEM((SUB, 2, piece, near_cols), BF),
+            pltpu.VMEM((nx, LANES, row_cols), BF),
+            pltpu.VMEM((width, row_cols), BF),
             pltpu.VMEM(((nx - 1) * LANES, width), BF),
             pltpu.VMEM((nx - 1, LANES, width), BF),
-            pltpu.VMEM((width, cols), BF),
+            pltpu.VMEM((width, 2 * cols - near_cols), BF),
             pltpu.VMEM((LANES, width), BF),
             pltpu.VMEM((LANES, width), BF),
             pltpu.VMEM((SUB, 2 * piece, width), BF),
@@ -763,7 +799,7 @@
             dma((len(arrays),)), dma((4,)), dma((5,)), dma((5,)), dma((SUB, 4)), dma((SUB,)), dma((2,)), dma((2,)),
             dma((2,)), dma((SUB,)), dma((SUB,)), dma((SUB, 4)), dma, dma((2,)), dma((2,)), dma((2,)),
             dma((4,)), dma, dma((4,)), dma((4,)), dma,
-            dma((4,)), dma, dma((2,)), dma((2,)), dma((8,)), dma, dma((nx,)), dma,
+            dma((4,)), dma, dma((3,)), dma((6,)), dma((8,)), dma, dma((nx,)), dma,
         ],
         compiler_params=pltpu.CompilerParams(
             collective_id=0, has_side_effects=True, vmem_limit_bytes=VMEM_LIMIT

time: 79.5 us -> 83.2 us (1.047)
  Pallas kernels: 76 us -> 79.3 us
    pallas_call x1, Pallas kernels: 74 us -> 77.4 us  [local(): pl.pallas_call(functools.partial(kernel, n), out_shape=(jax.ShapeDtypeStr...]
where the time goes in v7:
time: 83.2 us; the launch traced here: 81.9 us
  Pallas kernels  79.3 us (95%)
  between operations  2.58 us (3%)
    pallas_call x1, Pallas kernels, local(): pl.pallas_call(functools.partial(kernel, n), out_shape=(jax.ShapeDtypeStr...  77.4 us
    pallas_call x1, Pallas kernels, local(): pl.pallas_call(functools.partial(finish_kernel, n // (2 * nx)), out_shape...  1.96 us

profile of v7, /device:TPU:6, one launch (start us, length us, event | category | flops | bytes accessed | tf_op | source)
XLA Modules:
  0.0 81.9 jit_solution(3038457098515359790)
XLA Ops:
  2.6 77.4 %shard_map.208 = (bf16[128,256]{1,0:T(8,128)(2,1)}, bf16[128,256]{1,0:T(8,128)(2,1)}, f32[128,256]{1,0:T(8,128)}, bf16[1152,128]{1,0:T(8,128)(2,1)}) custom-call(s32[1]{0:T(128)S(6)} %copy.23.index_ref, s32[1]{0:T(128)S(6)} %copy.24.rank_ref, s32[1]{0:T(128)S(6)} %copy.25.length_ref, bf16[128,256]{1,0:T(8,128)(2,1)} %bitcast.10, bf16[128,256]{1,0:T(8,128)(2,1)} %bitcast.11, ...), custom_call_target="tpu_custom_call" | custom-call | tf_op jit(solution)/shard_map/pallas_call | solution.py:755
  79.9 2.0 %shard_map.209 = (bf16[128,256]{1,0:T(8,128)(2,1)}, bf16[128,256]{1,0:T(8,128)(2,1)}, f32[128,256]{1,0:T(8,128)}, f32[1,256]{1,0:T(1,128)}, f32[2,16,256]{2,1,0:T(8,128)}, /*index=5*/f32[2,16,4096]{2,1,0:T(8,128)}) custom-call(bf16[128,256]{1,0:T(8,128)(2,1)} %get-tuple-element.16.gsig_in, bf16[128,256]{1,0:T(8,128)(2,1)} %get-tuple-element.17.ggat_in, ...), custom_call_target="tpu_custom_call" | custom-call | tf_op jit(solution)/shard_map/pallas_call | solution.py:808

commit v8 on v6

--- a/solution.py
+++ b/solution.py
@@ -88,7 +88,7 @@
     in_sem, out_sem, a2a_send_sem, a2a_recv_sem, m_send_sem, m_recv_sem, own_sem, w_sem, pre0_sem,
     pre_send_sem, pre_recv_sem, ret_send_sem, ret_recv_sem, d_sem, r_sem, b_sem,
     q_send_sem, q_recv_sem, g_sem, f_send_sem, f_recv_sem,
-    h_send_sem, h_recv_sem, far_sem, wf_sem, wy_send_sem, wy_recv_sem, fr_send_sem, fr_recv_sem,
+    h_send_sem, h_recv_sem, far_sem, half_sem, wf_sem, wy_send_sem, wy_recv_sem, fr_send_sem, fr_recv_sem,
 ):
     dp = lax.axis_index("dp")
     me = lax.axis_index("seq")
@@ -249,15 +249,22 @@
     )
     wf_copy.start()
 
+    half_rows = LANES // 2
+
+    def rows_of_core(c):
+        return pl.ds(pl.multiple_of(c * half_rows, half_rows), half_rows)
+
     def far_copy(d, c):
         k = lax.rem(x + d, nx)
+        core = lax.rem(ch + c, 2)
         at = lax.rem(far, 2) * 2 * cols + k * far_cols
-        src = cot_hbm.at[:, pl.ds(pl.multiple_of(at, far_cols), far_cols)]
+        src = cot_hbm.at[rows_of_core(core), pl.ds(pl.multiple_of(at, far_cols), far_cols)]
+        dst = m_far.at[d, rows_of_core(core)]
         if d == 0 and c == 0:
-            return pltpu.make_async_copy(src, m_far.at[d], far_sem.at[1])
+            return pltpu.make_async_copy(src, dst, far_sem.at[1])
         return pltpu.make_async_remote_copy(
-            src_ref=src, dst_ref=m_far.at[d], send_sem=far_sem.at[0], recv_sem=far_sem.at[1],
-            device_id=(dp, member(zl * nx + k), lax.rem(ch + c, 2)), device_id_type=MESH,
+            src_ref=src, dst_ref=dst, send_sem=far_sem.at[0], recv_sem=far_sem.at[1],
+            device_id=(dp, member(zl * nx + k), core), device_id_type=MESH,
         )
 
     holds_far = ch == lax.div(far, 2)
@@ -363,6 +370,13 @@
     def gather_channels(src):
         return jnp.concatenate([src[:, cc, :] for cc in range(PER)], axis=0)
 
+    part = m_far.at[:, pl.ds(0, half_rows)]
+    pltpu.make_async_copy(part, part, far_sem.at[1]).wait()
+    half_copy = to_chan(
+        m_far.at[:, rows_of_core(ch)], m_far.at[:, rows_of_core(ch)], half_sem.at[0], half_sem.at[1]
+    )
+    half_copy.start()
+
     a2a_wait(0, sf_recv)
     forward(lambda cc: sf_recv[pl.ds(cc, n, stride=8), :], spec_s)
     forward(lambda cc: sf_recv[pl.ds(PER + cc, n, stride=8), :], spec_f)
@@ -374,7 +388,7 @@
     d_copy.wait()
     back_rank = (2.0 * (d_send[...] + d_recv[...]) * keep).astype(BF)
 
-    pltpu.make_async_copy(m_far, m_far, far_sem.at[1]).wait()
+    half_copy.wait_recv()
     if ny > 1:
         rest = w_far.at[pl.ds(0, (ny - 1) * slice_rows), :]
         pltpu.make_async_copy(rest, rest, wy_recv_sem).wait()
@@ -597,13 +611,15 @@
     w_copy.wait_send()
     pre0_copy.wait_send()
     wf_copy.wait_send()
+    half_copy.wait_send()
     for copy in wy_copies + far_copies + pre_copies + ret_copies + f_copies + h_copies:
         copy.wait_send()
 
     @pl.when(holds_far)
     def _():
         def sent(d, _):
-            pltpu.make_async_copy(m_far.at[0], m_far.at[0], far_sem.at[0]).wait()
+            part = m_far.at[0, pl.ds(0, half_rows)]
+            pltpu.make_async_copy(part, part, far_sem.at[0]).wait()
             return 0
 
         lax.fori_loop(1, 2 * nx, sent, 0)
@@ -763,7 +779,7 @@
             dma((len(arrays),)), dma((4,)), dma((5,)), dma((5,)), dma((SUB, 4)), dma((SUB,)), dma((2,)), dma((2,)),
             dma((2,)), dma((SUB,)), dma((SUB,)), dma((SUB, 4)), dma, dma((2,)), dma((2,)), dma((2,)),
             dma((4,)), dma, dma((4,)), dma((4,)), dma,
-            dma((4,)), dma, dma((2,)), dma((2,)), dma((8,)), dma, dma((nx,)), dma,
+            dma((4,)), dma, dma((2,)), dma((2,)), dma((2,)), dma((8,)), dma, dma((nx,)), dma,
         ],
         compiler_params=pltpu.CompilerParams(
             collective_id=0, has_side_effects=True, vmem_limit_bytes=VMEM_LIMIT

time: 79.5 us -> 79.9 us (level)
  Pallas kernels: 76 us -> 76.8 us
    pallas_call x1, Pallas kernels: 74 us -> 74.8 us  [local(): pl.pallas_call(functools.partial(kernel, n), out_shape=(jax.ShapeDtypeStr...]
where the time goes in v8:
time: 79.9 us; the launch traced here: 79.4 us
  Pallas kernels  76.8 us (96%)
  between operations  2.58 us (3%)
    pallas_call x1, Pallas kernels, local(): pl.pallas_call(functools.partial(kernel, n), out_shape=(jax.ShapeDtypeStr...  74.8 us
    pallas_call x1, Pallas kernels, local(): pl.pallas_call(functools.partial(finish_kernel, n // (2 * nx)), out_shape...  1.96 us

profile of v8, /device:TPU:6, one launch (start us, length us, event | category | flops | bytes accessed | tf_op | source)
XLA Modules:
  0.0 79.4 jit_solution(2880764737387753975)
XLA Ops:
  2.6 74.8 %shard_map.208 = (bf16[128,256]{1,0:T(8,128)(2,1)}, bf16[128,256]{1,0:T(8,128)(2,1)}, f32[128,256]{1,0:T(8,128)}, bf16[1152,128]{1,0:T(8,128)(2,1)}) custom-call(s32[1]{0:T(128)S(6)} %copy.23.index_ref, s32[1]{0:T(128)S(6)} %copy.24.rank_ref, s32[1]{0:T(128)S(6)} %copy.25.length_ref, bf16[128,256]{1,0:T(8,128)(2,1)} %bitcast.10, bf16[128,256]{1,0:T(8,128)(2,1)} %bitcast.11, ...), custom_call_target="tpu_custom_call" | custom-call | tf_op jit(solution)/shard_map/pallas_call | solution.py:735
  77.4 2.0 %shard_map.209 = (bf16[128,256]{1,0:T(8,128)(2,1)}, bf16[128,256]{1,0:T(8,128)(2,1)}, f32[128,256]{1,0:T(8,128)}, f32[1,256]{1,0:T(1,128)}, f32[2,16,256]{2,1,0:T(8,128)}, /*index=5*/f32[2,16,4096]{2,1,0:T(8,128)}) custom-call(bf16[128,256]{1,0:T(8,128)(2,1)} %get-tuple-element.16.gsig_in, bf16[128,256]{1,0:T(8,128)(2,1)} %get-tuple-element.17.ggat_in, ...), custom_call_target="tpu_custom_call" | custom-call | tf_op jit(solution)/shard_map/pallas_call | solution.py:788

commit v9 on v6

--- a/solution.py
+++ b/solution.py
@@ -194,8 +194,6 @@
     def block(j):
         return j
 
-    a2a_start(0, sf_send, sf_recv, eight)
-
     def cot_copy(sub, qq, hh):
         q = 2 * ch + qq
         return pltpu.make_async_remote_copy(
@@ -226,6 +224,8 @@
                 @pl.when(to_other(qq))
                 def _():
                     cot_copy(sub, qq, hh).start()
+    a2a_start(0, sf_send, sf_recv, eight)
+
     for qq in range(2):
         for hh in range(2):
             @pl.when((2 * ch + qq == dp) & (ch != hh))

time: 79.5 us -> 79.6 us (level)
  no operation moved by 1% of the time
where the time goes in v9:
time: 79.6 us; the launch traced here: 79 us
  Pallas kernels  76.4 us (96%)
  between operations  2.58 us (3%)
    pallas_call x1, Pallas kernels, local(): pl.pallas_call(functools.partial(kernel, n), out_shape=(jax.ShapeDtypeStr...  74.5 us
    pallas_call x1, Pallas kernels, local(): pl.pallas_call(functools.partial(finish_kernel, n // (2 * nx)), out_shape...  1.96 us

profile of v9, /device:TPU:6, one launch (start us, length us, event | category | flops | bytes accessed | tf_op | source)
XLA Modules:
  0.0 79.0 jit_solution(808478423032422157)
XLA Ops:
  2.6 74.5 %shard_map.208 = (bf16[128,256]{1,0:T(8,128)(2,1)}, bf16[128,256]{1,0:T(8,128)(2,1)}, f32[128,256]{1,0:T(8,128)}, bf16[1152,128]{1,0:T(8,128)(2,1)}) custom-call(s32[1]{0:T(128)S(6)} %copy.23.index_ref, s32[1]{0:T(128)S(6)} %copy.24.rank_ref, s32[1]{0:T(128)S(6)} %copy.25.length_ref, bf16[128,256]{1,0:T(8,128)(2,1)} %bitcast.10, bf16[128,256]{1,0:T(8,128)(2,1)} %bitcast.11, ...), custom_call_target="tpu_custom_call" | custom-call | tf_op jit(solution)/shard_map/pallas_call | solution.py:719
  77.0 2.0 %shard_map.209 = (bf16[128,256]{1,0:T(8,128)(2,1)}, bf16[128,256]{1,0:T(8,128)(2,1)}, f32[128,256]{1,0:T(8,128)}, f32[1,256]{1,0:T(1,128)}, f32[2,16,256]{2,1,0:T(8,128)}, /*index=5*/f32[2,16,4096]{2,1,0:T(8,128)}) custom-call(bf16[128,256]{1,0:T(8,128)(2,1)} %get-tuple-element.16.gsig_in, bf16[128,256]{1,0:T(8,128)(2,1)} %get-tuple-element.17.ggat_in, ...), custom_call_target="tpu_custom_call" | custom-call | tf_op jit(solution)/shard_map/pallas_call | solution.py:772
